TPU v7x, 512 devices: a whole 4x8x8 slice. The times are simulated.
512 devices in a mesh: slide: 64 (over z, x, core), seq: 8 (over y).
Axes of the slice: x: 4, y: 8, z: 8, core: 2. Of those that a mesh axis runs over, the one named last changes fastest.
Arguments:
- queries: bfloat16 [131072, 768], P(('slide', 'seq')), may hold values from -120 to 120
- keys: bfloat16 [131072, 768], P(('slide', 'seq')), may hold values from -4 to 4
- values: bfloat16 [131072, 768], P(('slide', 'seq')), may hold values from -6 to 6
- grad_y: bfloat16 [131072, 768], P(('slide', 'seq')), may hold values from -24 to 24
- lengths: int32 [64], P('slide'), may hold values from 512 to 2048, as said below
- w_out: bfloat16 [768, 768], replicated, may hold values from -0.21875 to 0.21875
Outputs:
- output: bfloat16 [131072, 768], P(('slide', 'seq'))
- grad_q: bfloat16 [131072, 768], P(('slide', 'seq'))
- grad_k: bfloat16 [131072, 768], P(('slide', 'seq'))
- grad_v: bfloat16 [131072, 768], P(('slide', 'seq'))
- weight_grad: float32 [768, 768], P('seq', 'slide')
Inputs may be any that keep to these rules, and one draw needn't show every extreme that they name: `lengths`: each slide's tile count; some slide holds all 2048 positions.
All inputs are finite; a program needn't handle non-finite values.
Results may differ from a plain program's by a relative error of at most 0.035.
Values may be sent and summed in bfloat16 or wider, within the bound.
A program may use at most 64 MiB of HBM per device.

v0:
```python
import jax
import jax.numpy as jnp
import numpy as np
from jax import lax
from jax.sharding import PartitionSpec as P

HEAD_COUNT = 12
HD = 64
D = 768
DILATION_STEP = 16


masked_score = -1e30


def pick_rows(array_input):
    reshaped_rows = array_input.reshape(
        (array_input.shape[0] // DILATION_STEP, DILATION_STEP) + array_input.shape[1:]
    )
    return reshaped_rows[:, np.arange(HEAD_COUNT) % DILATION_STEP, np.arange(HEAD_COUNT)]


def spread_rows(array_input, filler):
    choose_rows = (
        np.arange(DILATION_STEP)[:, None] == (np.arange(HEAD_COUNT) % DILATION_STEP)[None, :]
    )
    choose_rows = choose_rows.reshape(
        (1, DILATION_STEP, HEAD_COUNT) + (1,) * (array_input.ndim - 2)
    )
    scatter_rows = jnp.where(
        choose_rows, array_input[:, None], jnp.asarray(filler, array_input.dtype)
    )
    return scatter_rows.reshape((array_input.shape[0] * DILATION_STEP,) + array_input.shape[1:])


def body(queries, keys, values, grad_y, lengths, w_out):
    f32 = jnp.float32
    row_number_total = queries.shape[0]
    chosen_count = row_number_total // DILATION_STEP
    seq_count = lax.axis_size("seq")
    score_scale = HD ** (-0.5)
    row_start = lax.axis_index("seq") * row_number_total
    length = lengths[0]
    position = row_start + jnp.arange(row_number_total, dtype=jnp.int32)
    row_valid = position < length
    q_heads = queries.reshape(row_number_total, HEAD_COUNT, HD)
    k_heads = keys.reshape(row_number_total, HEAD_COUNT, HD)
    v_heads = values.reshape(row_number_total, HEAD_COUNT, HD)
    dense_score = (
        jnp.einsum("ihd,jhd->hij", q_heads, k_heads, preferred_element_type=f32) * score_scale
    )
    dense_score = jnp.where(row_valid[None, None, :], dense_score, masked_score)
    dense_max = dense_score.max(-1)
    q_sel = pick_rows(q_heads)
    k_sel = pick_rows(k_heads)
    v_sel = pick_rows(v_heads)
    k_far, v_far = (
        lax.all_gather(k_sel, "seq", axis=0, tiled=True),
        lax.all_gather(v_sel, "seq", axis=0, tiled=True),
    )
    distant_index = jnp.arange(chosen_count * seq_count, dtype=jnp.int32)
    head_displacement = jnp.asarray(np.arange(HEAD_COUNT) % DILATION_STEP, jnp.int32)
    distant_location = (
        distant_index // chosen_count * row_number_total
        + distant_index % chosen_count * DILATION_STEP
    )[:, None] + head_displacement[None, :]
    far_valid = distant_location < length
    sel_valid = pick_rows(jnp.broadcast_to(row_valid[:, None], (row_number_total, HEAD_COUNT)))
    sparse_score = (
        jnp.einsum("ahd,bhd->hab", q_sel, k_far, preferred_element_type=f32) * score_scale
    )
    sparse_score = jnp.where(far_valid.T[:, None, :], sparse_score, masked_score)
    sparse_max = sparse_score.max(-1)
    row_max = jnp.maximum(dense_max.T, spread_rows(sparse_max.T, masked_score))
    max_sel = pick_rows(row_max)
    dense_exp = jnp.where(
        row_valid[None, None, :], jnp.exp(dense_score - row_max.T[:, :, None]), 0.0
    )
    sparse_exp = jnp.where(
        far_valid.T[:, None, :], jnp.exp(sparse_score - max_sel.T[:, :, None]), 0.0
    )
    row_total = dense_exp.sum(-1).T + spread_rows(sparse_exp.sum(-1).T, 0.0)
    row_total = jnp.where(row_valid[:, None], row_total, 1.0)
    total_sel = pick_rows(row_total)
    dense_prob = jnp.where(row_valid[None, :, None], dense_exp / row_total.T[:, :, None], 0.0)
    sparse_prob = jnp.where(sel_valid.T[:, :, None], sparse_exp / total_sel.T[:, :, None], 0.0)
    dense_half = dense_prob.astype(jnp.bfloat16)
    sparse_half = sparse_prob.astype(jnp.bfloat16)
    dense_out = jnp.einsum("hij,jhd->ihd", dense_half, v_heads, preferred_element_type=f32)
    sparse_out = jnp.einsum("hab,bhd->ahd", sparse_half, v_far, preferred_element_type=f32)
    attended = (dense_out + spread_rows(sparse_out, 0.0)).astype(jnp.bfloat16)
    attn_flat = attended.reshape(row_number_total, D)
    output = jnp.dot(attn_flat, w_out, preferred_element_type=f32).astype(jnp.bfloat16)
    grad_attn = lax.dot_general(
        grad_y, w_out, (((1,), (1,)), ((), ())), preferred_element_type=f32
    ).astype(jnp.bfloat16)
    weight_part = lax.dot_general(
        attn_flat, grad_y, (((0,), (0,)), ((), ())), preferred_element_type=f32
    )
    grad_heads = grad_attn.reshape(row_number_total, HEAD_COUNT, HD)
    row_dot = jnp.sum(grad_heads.astype(f32) * attended.astype(f32), axis=-1)
    dot_sel = pick_rows(row_dot)
    dense_dprob = jnp.einsum("ihd,jhd->hij", grad_heads, v_heads, preferred_element_type=f32)
    dense_dscore = (dense_prob * (dense_dprob - row_dot.T[:, :, None])).astype(jnp.bfloat16)
    grad_q_dense = (
        jnp.einsum("hij,jhd->ihd", dense_dscore, k_heads, preferred_element_type=f32) * score_scale
    )
    grad_k_dense = (
        jnp.einsum("hij,ihd->jhd", dense_dscore, q_heads, preferred_element_type=f32) * score_scale
    )
    grad_v_dense = jnp.einsum("hij,ihd->jhd", dense_half, grad_heads, preferred_element_type=f32)
    grad_sel = pick_rows(grad_heads)
    sparse_dprob = jnp.einsum("ahd,bhd->hab", grad_sel, v_far, preferred_element_type=f32)
    sparse_dscore = (sparse_prob * (sparse_dprob - dot_sel.T[:, :, None])).astype(jnp.bfloat16)
    grad_q_sparse = (
        jnp.einsum("hab,bhd->ahd", sparse_dscore, k_far, preferred_element_type=f32) * score_scale
    )
    key_part = (
        jnp.einsum("hab,ahd->bhd", sparse_dscore, q_sel, preferred_element_type=f32) * score_scale
    )
    value_part = jnp.einsum("hab,ahd->bhd", sparse_half, grad_sel, preferred_element_type=f32)
    grad_k_sparse, grad_v_sparse = (
        lax.psum_scatter(key_part, "seq", scatter_dimension=0, tiled=True),
        lax.psum_scatter(value_part, "seq", scatter_dimension=0, tiled=True),
    )
    grad_q = (
        (grad_q_dense + spread_rows(grad_q_sparse, 0.0))
        .astype(jnp.bfloat16)
        .reshape(row_number_total, D)
    )
    grad_k = (
        (grad_k_dense + spread_rows(grad_k_sparse, 0.0))
        .astype(jnp.bfloat16)
        .reshape(row_number_total, D)
    )
    grad_v = (
        (grad_v_dense + spread_rows(grad_v_sparse, 0.0))
        .astype(jnp.bfloat16)
        .reshape(row_number_total, D)
    )
    over_slides = lax.psum_scatter(weight_part, "slide", scatter_dimension=1, tiled=True)
    weight_grad = lax.psum_scatter(over_slides, "seq", scatter_dimension=0, tiled=True)
    return (output, grad_q, grad_k, grad_v, weight_grad)


def solution(mesh):
    return jax.shard_map(
        body,
        mesh=mesh,
        in_specs=(
            P(("slide", "seq"), None),
            P(("slide", "seq"), None),
            P(("slide", "seq"), None),
            P(("slide", "seq"), None),
            P("slide"),
            P(),
        ),
        out_specs=(
            P(("slide", "seq"), None),
            P(("slide", "seq"), None),
            P(("slide", "seq"), None),
            P(("slide", "seq"), None),
            P("seq", "slide"),
        ),
        check_vma=False,
    )
```

profile of v0, /device:TPU:1, one launch (start us, length us, event | category | flops | bytes accessed | tf_op | source)
XLA Modules:
  0.0 376.4 jit_solution(10675600939494724390)
XLA Ops:
  22.3 23.3 %all_gather.6 = bf16[128,12,64]{2,0,1:T(8,128)(2,1)} all-gather(bf16[16,12,64]{2,0,1:T(8,128)(2,1)S(1)} %bitcast.131), channel_id=1, replica_groups=mesh['slide'=64,'seq'=8] {'seq'}, dimensions={0}, use_global_device_ids=true | all-gather | bytes 221184 | tf_op jit(solution)/shard_map/all_gather | solution.py:58
  51.0 3.6 fusion.1
  55.8 2.7 fusion.2
  58.7 4.5 %divide_select_fusion = f32[12,256,256]{1,2,0:T(8,128)} fusion(f32[12,256,256]{1,2,0:T(8,128)} %get-tuple-element.23, f32[12,256]{1,0:T(8,128)S(1)} %bitcast.136, f32[12,256]{1,0:T(8,128)S(1)} %bitcast.134, pred[256]{0:T(512)(128)(4,1)S(1)} %add_compare_fusion.1), kind=kLoop, calls=%fused_computation.9 | loop fusion | flops 4718592 | bytes 6316288 | tf_op jit(solution)/shard_map/jit(_where)/select_n | solution.py:85
  65.8 19.1 %all_gather.7 = bf16[128,12,64]{2,0,1:T(8,128)(2,1)S(1)} all-gather(bf16[16,12,64]{2,0,1:T(8,128)(2,1)S(1)} %bitcast.132), channel_id=1, replica_groups=mesh['slide'=64,'seq'=8] {'seq'}, dimensions={0}, use_global_device_ids=true | all-gather | bytes 221184 | tf_op jit(solution)/shard_map/all_gather | solution.py:59
  88.5 3.0 multiply_reduce_fusion
  93.8 88.1 %fusion = f32[768,16]{0,1:T(8,128)} fusion(f32[768,768]{0,1:T(8,128)S(1)} %fusion.37), kind=kCustom, calls=%all-reduce-scatter | all-reduce-scatter fusion | flops 786433 | bytes 2410496
  184.9 3.7 collective-permute-start
  188.6 2.8 collective-permute-start.1
  191.4 4.5 %collective-permute-start.10 = (f32[768,16]{0,1:T(8,128)}, f32[768,16]{0,1:T(8,128)S(1)}, u32[]{:S(2)}, u32[]{:S(2)}) collective-permute-start(f32[768,16]{0,1:T(8,128)} %fusion), channel_id=1, source_target_pairs={{0,88},{8,96},{16,104},{24,112},{32,120},{40,128},{48,136},{56,144... | collective-permute-start | bytes 147464
  195.9 4.6 %collective-permute-start.11 = (f32[768,16]{0,1:T(8,128)}, f32[768,16]{0,1:T(8,128)S(1)}, u32[]{:S(2)}, u32[]{:S(2)}) collective-permute-start(f32[768,16]{0,1:T(8,128)} %fusion), channel_id=1, source_target_pairs={{0,96},{8,104},{16,112},{24,120},{32,128},{40,136},{48,144},{56,15... | collective-permute-start | bytes 147464
  200.5 5.3 %collective-permute-start.12 = (f32[768,16]{0,1:T(8,128)}, f32[768,16]{0,1:T(8,128)S(1)}, u32[]{:S(2)}, u32[]{:S(2)}) collective-permute-start(f32[768,16]{0,1:T(8,128)} %fusion), channel_id=1, source_target_pairs={{0,104},{8,112},{16,120},{24,128},{32,136},{40,144},{48,152},{56,1... | collective-permute-start | bytes 147464
  209.1 3.5 collective-permute-start.2
  212.6 3.6 collective-permute-start.3
  217.9 2.9 collective-permute-start.5
  220.8 3.2 collective-permute-start.6
  235.1 9.5 %concatenate.48 = f32[768,268]{0,1:T(8,128)S(1)} concatenate(f32[768,12]{0,1:T(8,128)S(1)} %collective-permute-done.15, f32[768,16]{0,1:T(8,128)} %copy-done.24, f32[768,16]{0,1:T(8,128)} %copy-done.23, f32[768,16]{0,1:T(8,128)S(1)} %collective-permute-done.12, f32[768,16]{0,1:T(8,128)S(1)} %collective-permute-done.11, f32[768,16]{0,1:T(8,128)S(1)} %collective-permute-done.10, ...), dimensions={1} | concatenate | bytes 1646592
  255.3 2.8 copy.107
  264.5 10.9 %reduce-scatter.12.cloned.1.call-done = f32[96,12]{1,0:T(8,128)} async-done(((f32[768,12]{1,0:T(8,128)}), f32[96,12]{1,0:T(8,128)}) %reduce-scatter.12.cloned.1.call-update) | async-done | bytes 4624
  276.9 42.2 %reduce-scatter.10.cloned.1.call-done = f32[16,12,64]{2,1,0:T(8,128)} async-done(((f32[128,12,64]{2,1,0:T(8,128)}), f32[16,12,64]{2,1,0:T(8,128)}) %reduce-scatter.10.cloned.1.call-update) | async-done | bytes 49168 | tf_op jit(solution)/shard_map/reduce_scatter | solution.py:124
  321.3 2.8 copy.115
  324.0 2.7 fusion.11
  327.7 34.6 %reduce-scatter.8.cloned.1.call-done = f32[16,12,64]{2,1,0:T(8,128)} async-done(((f32[128,12,64]{2,1,0:T(8,128)}), f32[16,12,64]{2,1,0:T(8,128)}) %reduce-scatter.8.cloned.1.call-update) | async-done | bytes 49168 | tf_op jit(solution)/shard_map/reduce_scatter | solution.py:123
  364.5 2.7 copy.111
  (171 shorter events, 74.3 us)
Async XLA Ops:
  7.2 80.2 %copy-start = (bf16[768,768]{1,0:T(8,128)(2,1)S(1)}, bf16[768,768]{1,0:T(8,128)(2,1)}, u32[]{:S(2)}) copy-start(bf16[768,768]{1,0:T(8,128)(2,1)} %param.50) | copy-start | bytes 3538948
  7.2 268.2 %reduce-scatter.12.cloned.1.call-start = ((), (), s32[]{:S(2)}) async-start(), calls=%async_computation.5 | async-start | bytes 442368
  181.9 63.8 %copy-start.19 = (f32[12,16,128]{2,1,0:T(8,128)S(1)}, f32[12,16,128]{2,1,0:T(8,128)}, u32[]{:S(2)}) copy-start(f32[12,16,128]{2,1,0:T(8,128)} %copy-done.18) | copy-start | bytes 294916
  181.9 63.8 %copy-start.29 = (pred[12,128]{1,0:T(8,128)(4,1)S(1)}, pred[12,128]{1,0:T(8,128)(4,1)}, u32[]{:S(2)}) copy-start(pred[12,128]{1,0:T(8,128)(4,1)} %copy-done.28) | copy-start | bytes 4612
  181.9 63.8 %copy-start.33 = (f32[12,16]{1,0:T(8,128)S(1)}, f32[12,16]{1,0:T(8,128)}, u32[]{:S(2)}) copy-start(f32[12,16]{1,0:T(8,128)} %copy-done.32) | copy-start | bytes 2308
  181.9 63.8 %copy-start.35 = (pred[12,16]{1,0:T(8,128)(4,1)S(1)}, pred[12,16]{1,0:T(8,128)(4,1)}, u32[]{:S(2)}) copy-start(pred[12,16]{1,0:T(8,128)(4,1)} %copy-done.34) | copy-start | bytes 580
  182.8 17.8 %collective-permute-start.15 = (f32[768,12]{0,1:T(8,128)S(1)}, f32[768,12]{0,1:T(8,128)S(1)}, u32[]{:S(2)}, u32[]{:S(2)}) collective-permute-start(f32[768,12]{0,1:T(8,128)S(1)} %slice.16), channel_id=1, source_target_pairs={{0,128},{8,136},{16,144},{24,152},{32,160},{40,168},{48,176},{56,1... | collective-permute-start | bytes 110600
  184.9 21.0 %collective-permute-start = (f32[768,16]{0,1:T(8,128)}, f32[768,16]{0,1:T(8,128)S(1)}, u32[]{:S(2)}, u32[]{:S(2)}) collective-permute-start(f32[768,16]{0,1:T(8,128)} %fusion), channel_id=1, source_target_pairs={{0,8},{8,16},{16,24},{24,32},{32,40},{40,48},{48,56},{56,64},{64,7... | collective-permute-start | bytes 147464
  188.6 18.6 %collective-permute-start.1 = (f32[768,16]{0,1:T(8,128)}, f32[768,16]{0,1:T(8,128)S(1)}, u32[]{:S(2)}, u32[]{:S(2)}) collective-permute-start(f32[768,16]{0,1:T(8,128)} %fusion), channel_id=1, source_target_pairs={{0,16},{8,24},{16,32},{24,40},{32,48},{40,56},{48,64},{56,72},{64,... | collective-permute-start | bytes 147464
  191.4 17.7 %collective-permute-start.10 = (f32[768,16]{0,1:T(8,128)}, f32[768,16]{0,1:T(8,128)S(1)}, u32[]{:S(2)}, u32[]{:S(2)}) collective-permute-start(f32[768,16]{0,1:T(8,128)} %fusion), channel_id=1, source_target_pairs={{0,88},{8,96},{16,104},{24,112},{32,120},{40,128},{48,136},{56,144... | collective-permute-start | bytes 147464
  195.9 16.7 %collective-permute-start.11 = (f32[768,16]{0,1:T(8,128)}, f32[768,16]{0,1:T(8,128)S(1)}, u32[]{:S(2)}, u32[]{:S(2)}) collective-permute-start(f32[768,16]{0,1:T(8,128)} %fusion), channel_id=1, source_target_pairs={{0,96},{8,104},{16,112},{24,120},{32,128},{40,136},{48,144},{56,15... | collective-permute-start | bytes 147464
  200.5 15.7 %collective-permute-start.12 = (f32[768,16]{0,1:T(8,128)}, f32[768,16]{0,1:T(8,128)S(1)}, u32[]{:S(2)}, u32[]{:S(2)}) collective-permute-start(f32[768,16]{0,1:T(8,128)} %fusion), channel_id=1, source_target_pairs={{0,104},{8,112},{16,120},{24,128},{32,136},{40,144},{48,152},{56,1... | collective-permute-start | bytes 147464
  205.9 12.0 %collective-permute-start.13 = (f32[768,16]{0,1:T(8,128)}, f32[768,16]{0,1:T(8,128)S(1)}, u32[]{:S(2)}, u32[]{:S(2)}) collective-permute-start(f32[768,16]{0,1:T(8,128)} %fusion), channel_id=1, source_target_pairs={{0,112},{8,120},{16,128},{24,136},{32,144},{40,152},{48,160},{56,1... | collective-permute-start | bytes 147464
  207.3 13.5 %collective-permute-start.14 = (f32[768,16]{0,1:T(8,128)}, f32[768,16]{0,1:T(8,128)S(1)}, u32[]{:S(2)}, u32[]{:S(2)}) collective-permute-start(f32[768,16]{0,1:T(8,128)} %fusion), channel_id=1, source_target_pairs={{0,120},{8,128},{16,136},{24,144},{32,152},{40,160},{48,168},{56,1... | collective-permute-start | bytes 147464
  209.1 14.8 %collective-permute-start.2 = (f32[768,16]{0,1:T(8,128)}, f32[768,16]{0,1:T(8,128)S(1)}, u32[]{:S(2)}, u32[]{:S(2)}) collective-permute-start(f32[768,16]{0,1:T(8,128)} %fusion), channel_id=1, source_target_pairs={{0,24},{8,32},{16,40},{24,48},{32,56},{40,64},{48,72},{56,80},{64,... | collective-permute-start | bytes 147464
  212.6 13.7 %collective-permute-start.3 = (f32[768,16]{0,1:T(8,128)}, f32[768,16]{0,1:T(8,128)S(1)}, u32[]{:S(2)}, u32[]{:S(2)}) collective-permute-start(f32[768,16]{0,1:T(8,128)} %fusion), channel_id=1, source_target_pairs={{0,32},{8,40},{16,48},{24,56},{32,64},{40,72},{48,80},{56,88},{64,... | collective-permute-start | bytes 147464
  216.2 12.0 %collective-permute-start.4 = (f32[768,16]{0,1:T(8,128)}, f32[768,16]{0,1:T(8,128)S(1)}, u32[]{:S(2)}, u32[]{:S(2)}) collective-permute-start(f32[768,16]{0,1:T(8,128)} %fusion), channel_id=1, source_target_pairs={{0,40},{8,48},{16,56},{24,64},{32,72},{40,80},{48,88},{56,96},{64,... | collective-permute-start | bytes 147464
  217.9 17.2 %collective-permute-start.5 = (f32[768,16]{0,1:T(8,128)}, f32[768,16]{0,1:T(8,128)}, u32[]{:S(2)}, u32[]{:S(2)}) collective-permute-start(f32[768,16]{0,1:T(8,128)} %fusion), channel_id=1, source_target_pairs={{0,48},{8,56},{16,64},{24,72},{32,80},{40,88},{48,96},{56,104},{64... | collective-permute-start | bytes 147464
  220.8 14.3 %collective-permute-start.6 = (f32[768,16]{0,1:T(8,128)}, f32[768,16]{0,1:T(8,128)}, u32[]{:S(2)}, u32[]{:S(2)}) collective-permute-start(f32[768,16]{0,1:T(8,128)} %fusion), channel_id=1, source_target_pairs={{0,56},{8,64},{16,72},{24,80},{32,88},{40,96},{48,104},{56,112},{6... | collective-permute-start | bytes 147464
  224.0 11.1 %collective-permute-start.7 = (f32[768,16]{0,1:T(8,128)}, f32[768,16]{0,1:T(8,128)}, u32[]{:S(2)}, u32[]{:S(2)}) collective-permute-start(f32[768,16]{0,1:T(8,128)} %fusion), channel_id=1, source_target_pairs={{0,64},{8,72},{16,80},{24,88},{32,96},{40,104},{48,112},{56,120},{... | collective-permute-start | bytes 147464
  226.3 8.7 %collective-permute-start.8 = (f32[768,16]{0,1:T(8,128)}, f32[768,16]{0,1:T(8,128)}, u32[]{:S(2)}, u32[]{:S(2)}) collective-permute-start(f32[768,16]{0,1:T(8,128)} %fusion), channel_id=1, source_target_pairs={{0,72},{8,80},{16,88},{24,96},{32,104},{40,112},{48,120},{56,128},... | collective-permute-start | bytes 147464
  228.3 6.8 %collective-permute-start.9 = (f32[768,16]{0,1:T(8,128)}, f32[768,16]{0,1:T(8,128)}, u32[]{:S(2)}, u32[]{:S(2)}) collective-permute-start(f32[768,16]{0,1:T(8,128)} %fusion), channel_id=1, source_target_pairs={{0,80},{8,88},{16,96},{24,104},{32,112},{40,120},{48,128},{56,136}... | collective-permute-start | bytes 147464
  245.6 73.4 %reduce-scatter.10.cloned.1.call-start = ((), (), s32[]{:S(2)}) async-start(), calls=%async_computation.4 | async-start | bytes 1179648 | tf_op jit(solution)/shard_map/reduce_scatter | solution.py:124
  247.5 114.7 %reduce-scatter.8.cloned.1.call-start = ((), (), s32[]{:S(2)}) async-start(), calls=%async_computation.3 | async-start | bytes 1179648 | tf_op jit(solution)/shard_map/reduce_scatter | solution.py:123
  (31 other events, 417.3 us)
Sparse Core Ops, SparseCore 0:
  245.8 29.5 reduce-scatter.11
  278.4 40.5 reduce-scatter.9
  322.1 40.0 reduce-scatter.7
where the time goes:
time: 382 us; the launch traced here: 376 us
  blocking collectives  130 us (34%)
  waiting for transfers between devices  87.7 us (23%)
  local copies, waits for them, and re-layouts  63.9 us (17%)
  starting transfers between devices  47.3 us (12%)
  matrix products  23.6 us (6%)
  between operations  15.8 us (4%)
  other arithmetic  7.62 us (2%)
    unnamed x1, blocking collectives  88.1 us
    unnamed x17, starting transfers between devices  47.2 us
    reduce_scatter x1, waiting for transfers between devices, body(): lax.psum_scatter(value_part, 'seq', scatter_dimension=0, tiled=True)  42.2 us
    reduce_scatter x1, waiting for transfers between devices, body(): lax.psum_scatter(key_part, 'seq', scatter_dimension=0, tiled=True)  34.6 us
    unnamed x84, local copies, waits for them, and re-layouts  24.7 us
    all_gather x1, blocking collectives, body(): lax.all_gather(k_sel, 'seq', axis=0, tiled=True)  23.3 us
    all_gather x1, blocking collectives, body(): lax.all_gather(v_sel, 'seq', axis=0, tiled=True)  19.1 us
    broadcast_in_dim x10, local copies, waits for them, and re-layouts, spread_rows(): jnp.where(choose_rows, array_input[:, None], jnp.asarray(filler, array_in...  13.7 us
  transfers between devices with their start and end apart: 19, of which 3 were waited for; matrix products, arithmetic and copies ran while one was open for 9% of the time, Pallas kernels for 0%

commit v1 on v0

v1 whole, which is shorter than its diff:
```python
import functools

import jax
import jax.numpy as jnp
from jax import lax
from jax.experimental import pallas as pl
from jax.experimental.pallas import tpu as pltpu
from jax.sharding import PartitionSpec as P

HEADS = 12
HD = 64
D = 768
ROWS = 256
STEP = 16
PICK = ROWS // STEP
COMPACT = HEADS * PICK
NY, NZ, NX = 8, 8, 4
FAR = NY * PICK
SCALE = HD**-0.5
NEG = -1e30
MESH = pl.DeviceIdType.MESH
bf16 = jnp.bfloat16
f32 = jnp.float32


def nn(a, b):
    return lax.dot_general(a, b, (((1,), (0,)), ((), ())), preferred_element_type=f32)


def nt(a, b):
    return lax.dot_general(a, b, (((1,), (1,)), ((), ())), preferred_element_type=f32)


def iota(shape, dim):
    return lax.broadcasted_iota(jnp.int32, shape, dim)


def half(cond):
    return jnp.where(cond, 1.0, 0.0).astype(bf16)


def kernel(
    len_ref, q_ref, k_ref, v_ref, gy_ref, w_ref,
    out_ref, gq_ref, gk_ref, gv_ref, wg_ref,
    kv_all, qg_all, aug_all, gyt, atth, att_far,
    grad, att, vt, kt, gk_acc, gv_acc,
    w_full, wy, wz, wx, r1y, r1z, r1x,
    a0, a1, a2, r20, r21, r22, s3, r3,
    kv_s, kv_r, qg_s, qg_r, aug_s, aug_r, core_s, core_r,
    y_s, y_r, z_s, z_r, x_s, x_r,
    b0_s, b0_r, b1_s, b1_r, b2_s, b2_r, f_s, f_r,
):
    slide = lax.axis_index("slide")
    y = lax.axis_index("seq")
    c = lax.rem(slide, 2)
    x = lax.rem(slide // 2, NX)
    z = slide // (2 * NX)

    def device(z_at, x_at, c_at, y_at):
        return ((z_at * NX + x_at) * 2 + c_at, y_at)

    def y_peer(d):
        return device(z, x, c, lax.rem(y + d, NY))

    def z_peer(d):
        return device(lax.rem(z + d, NZ), x, c, y)

    def x_peer(d):
        return device(z, lax.rem(x + d, NX), c, y)

    sibling = device(z, x, 1 - c, y)

    def send(src, dst, s_sem, r_sem, to):
        copy = pltpu.make_async_remote_copy(
            src_ref=src, dst_ref=dst, send_sem=s_sem, recv_sem=r_sem,
            device_id=to, device_id_type=MESH,
        )
        copy.start()
        return copy

    part = lax.rem(y, 4)
    src_c = y // 4

    def last_source(role, i):
        l = part - role
        at_y = jnp.where(l == 0, z, i)
        at_z = jnp.where(l == 0, i, jnp.where(l == 1, z, 4 * lax.rem(z, 2) + x))
        at_x = jnp.where(l == 2, z // 2, x)
        mine = (at_y == y) & (at_z == z) & (at_x == x) & (src_c == c)
        there = (l >= 0) & (l <= 2)
        return device(at_z, at_x, src_c, at_y), there, mine

    def last_target(l, role, c_to):
        to_y = 4 * c + l + role
        to_z = (y, z, 2 * x + z // 4)[l]
        to_x = (x, x, lax.rem(z, 4))[l]
        mine = (to_y == y) & (to_z == z) & (to_x == x) & (c == c_to)
        return device(to_z, to_x, c_to, to_y), mine

    r3[...] = jnp.zeros_like(r3)

    barrier = pltpu.get_barrier_semaphore()

    def greet(to):
        pl.semaphore_signal(barrier, inc=1, device_id=to, device_id_type=MESH)

    for d in range(1, NY):
        greet(y_peer(d))
    for d in range(1, NZ):
        greet(z_peer(d))
    for d in range(1, NX):
        greet(x_peer(d))
    greet(sibling)
    for role in range(2):

        def hail(i, carry, role=role):
            who, there, mine = last_source(role, i)

            @pl.when(there & jnp.logical_not(mine))
            def _():
                greet(who)

            return carry

        lax.fori_loop(0, NY, hail, 0)
    awaited = (NY - 1) + (NZ - 1) + (NX - 1) + 1
    for l in range(3):
        for role in range(2):
            for c_to in range(2):
                awaited = awaited + jnp.where(last_target(l, role, c_to)[1], 0, 1)

    length = len_ref[0]
    base = y * ROWS
    pick_mask = half(lax.rem(iota((ROWS, D), 0), STEP) == iota((ROWS, D), 1) // HD)
    squeeze = half(iota((PICK, ROWS), 1) // STEP == iota((PICK, ROWS), 0))

    def compact(rows):
        return nn(squeeze, rows * pick_mask).astype(bf16)

    k_sel = compact(k_ref[...])
    v_sel = compact(v_ref[...])
    kv_all[y, 0] = k_sel
    kv_all[y, 1] = v_sel
    gyt[0] = gy_ref[...].T

    pl.semaphore_wait(barrier, awaited)

    kv_copies = [
        send(kv_all.at[y], kv_all.at[y], kv_s.at[d - 1], kv_r.at[d - 1], y_peer(d))
        for d in (1, 7, 2, 6, 3, 5, 4)
    ]
    gyt_copy = send(gyt.at[0], gyt.at[1], core_s.at[0], core_r.at[0], sibling)

    grad[...] = nt(gy_ref[...], w_ref[...]).astype(bf16)
    q_sel = compact(q_ref[...]) * SCALE
    g_sel = compact(grad[...])
    qg_all[y, 0] = q_sel
    qg_all[y, 1] = g_sel
    qg_copies = [
        send(qg_all.at[y], qg_all.at[y], qg_s.at[d - 1], qg_r.at[d - 1], y_peer(d))
        for d in (1, 7, 2, 6, 3, 5, 4)
    ]

    vt[...] = v_ref[...].T
    kt[...] = (k_ref[...] * SCALE).T

    key_ok = base + iota((ROWS, 1), 0) < length
    query_at = iota((1, ROWS), 1)
    query_ok = base + query_at < length

    def pair(p, carry):
        cols = pl.ds(pl.multiple_of(p * 128, 128), 128)
        k2, v2, q2, g2 = k_ref[:, cols], v_ref[:, cols], q_ref[:, cols] * SCALE, grad[:, cols]
        gk2 = jnp.zeros((ROWS, 128), f32)
        gv2 = jnp.zeros((ROWS, 128), f32)
        tops = []
        for e in range(2):
            lanes = half(iota((1, 128), 1) // HD == e)
            own = pl.ds(pl.multiple_of(p * 128 + e * HD, HD), HD)
            q_one, g_one = q2 * lanes, g2 * lanes
            score = jnp.where(key_ok, nt(k2, q_one), NEG)
            ex = jnp.exp(score - jnp.max(score, axis=0, keepdims=True))
            total = jnp.sum(ex, axis=0, keepdims=True)
            used = query_ok & (lax.rem(query_at, STEP) != 2 * p + e)
            prob = ex * jnp.where(used, 1.0 / total, 0.0)
            prob_half = prob.astype(bf16)
            term = prob * nt(v2, g_one)
            dot = jnp.sum(term, axis=0, keepdims=True)
            dscore = (term - prob * dot).astype(bf16)
            tops.append((nn(vt[own, :], prob_half), nn(kt[own, :], dscore)))
            gk2 = gk2 + nn(dscore, q_one)
            gv2 = gv2 + nn(prob_half, g_one)
        att[:, cols] = jnp.concatenate([tops[0][0], tops[1][0]], axis=0).T
        gq_ref[:, cols] = jnp.concatenate([tops[0][1], tops[1][1]], axis=0).T.astype(bf16)
        gk_acc[:, cols] = gk2
        gv_acc[:, cols] = gv2
        return carry

    lax.fori_loop(0, D // 128, pair, 0)

    diagonal = half(iota((COMPACT, D), 0) // PICK == iota((COMPACT, D), 1) // HD)
    spread = half(
        (iota((ROWS, COMPACT), 0) // STEP == lax.rem(iota((ROWS, COMPACT), 1), PICK))
        & (lax.rem(iota((ROWS, COMPACT), 0), STEP) == iota((ROWS, COMPACT), 1) // PICK)
    )

    def block(rows):
        return jnp.concatenate([rows] * HEADS, axis=0) * diagonal

    def place(rows):
        return nn(spread, rows.astype(bf16) * diagonal)

    q_blk = block(q_sel)
    g_blk = block(g_sel)
    row = iota((COMPACT, 1), 0)
    sel_ok = base + lax.rem(row, PICK) * STEP + row // PICK < length
    far_at = (
        iota((COMPACT, FAR), 1) // PICK * ROWS
        + lax.rem(iota((COMPACT, FAR), 1), PICK) * STEP
        + iota((COMPACT, FAR), 0) // PICK
    )
    far_ok = far_at < length
    near_score = jnp.where(query_ok, nt(q_blk, k_ref[...]), NEG)
    near_dprob = nt(g_blk, v_ref[...])

    for copy in kv_copies:
        copy.wait_recv()
    k_far = kv_all[:, 0].reshape(FAR, D)
    v_far = kv_all[:, 1].reshape(FAR, D)

    far_score = jnp.where(far_ok, nt(q_blk, k_far), NEG)
    top = jnp.maximum(
        jnp.max(near_score, axis=1, keepdims=True), jnp.max(far_score, axis=1, keepdims=True)
    )
    near_ex = jnp.exp(near_score - top)
    far_ex = jnp.exp(far_score - top)
    total = jnp.sum(near_ex, axis=1, keepdims=True) + jnp.sum(far_ex, axis=1, keepdims=True)
    inv = jnp.where(sel_ok, 1.0 / total, 0.0)
    near_prob, far_prob = near_ex * inv, far_ex * inv
    near_half, far_half = near_prob.astype(bf16), far_prob.astype(bf16)
    sel_att = nn(near_half, v_ref[...]) + nn(far_half, v_far)
    attended = (att[...] + place(sel_att)).astype(bf16)
    atth[0] = attended[:, : D // 2]
    atth[1] = attended[:, D // 2 :]
    att_copy = send(atth.at[1 - c], att_far, core_s.at[1], core_r.at[1], sibling)

    near_term = near_prob * near_dprob
    far_term = far_prob * nt(g_blk, v_far)
    dot = jnp.sum(near_term, axis=1, keepdims=True) + jnp.sum(far_term, axis=1, keepdims=True)
    lse = jnp.where(sel_ok, top + jnp.log(total), 0.0)
    lane = iota((COMPACT, 128), 1)
    aug = jnp.zeros((COMPACT, 128), f32)
    for at, left in ((0, lse), (3, dot)):
        for n in range(3):
            top_bits = left.astype(bf16).astype(f32)
            aug = jnp.where(lane == (at + n) * STEP + row // PICK, top_bits, aug)
            left = left - top_bits
    aug_all[y] = jnp.sum(aug.reshape(HEADS, PICK, 128), axis=0).astype(bf16)
    aug_copies = [
        send(aug_all.at[y], aug_all.at[y], aug_s.at[d - 1], aug_r.at[d - 1], y_peer(d))
        for d in (1, 7, 2, 6, 3, 5, 4)
    ]

    out_ref[:, : D // 2] = (
        nn(atth[0], w_ref[: D // 2, : D // 2]) + nn(atth[1], w_ref[D // 2 :, : D // 2])
    ).astype(bf16)
    out_ref[:, D // 2 :] = (
        nn(atth[0], w_ref[: D // 2, D // 2 :]) + nn(atth[1], w_ref[D // 2 :, D // 2 :])
    ).astype(bf16)

    gyt_copy.wait_recv()
    att_copy.wait_recv()
    weight = nn(gyt[0], atth[c]) + nn(gyt[1], att_far[...])
    for l in range(3):
        w_full[l] = weight[:, l * 128 : (l + 1) * 128]
    wy[...] = w_full[0].reshape(NY, 96, 128).astype(bf16)
    wz[...] = w_full[1].reshape(NZ, 96, 128).astype(bf16)
    wx[...] = w_full[2].reshape(NX, 192, 128).astype(bf16)
    first = []
    for d in (4, 3, 5, 2, 6, 1, 7):
        first.append(
            send(wy.at[lax.rem(y + d, NY)], r1y.at[d - 1], y_s.at[d - 1], y_r.at[d - 1], y_peer(d))
        )
        first.append(
            send(wz.at[lax.rem(z + d, NZ)], r1z.at[d - 1], z_s.at[d - 1], z_r.at[d - 1], z_peer(d))
        )
        if d < NX:
            first.append(
                send(wx.at[lax.rem(x + d, NX)], r1x.at[d - 1], x_s.at[d - 1], x_r.at[d - 1], x_peer(d))
            )

    near_ds = (near_term - near_prob * dot).astype(bf16)
    far_ds = (far_term - far_prob * dot).astype(bf16)
    sel_gq = (nn(near_ds, k_ref[...]) + nn(far_ds, k_far)) * SCALE
    gq_ref[...] = gq_ref[...] + place(sel_gq).astype(bf16)
    gk_acc[...] += nn(near_ds.astype(f32).T.astype(bf16), q_blk)
    gv_acc[...] += nn(near_prob.T.astype(bf16), g_blk)

    for copy in qg_copies:
        copy.wait_recv()
    for copy in aug_copies:
        copy.wait_recv()
    q_far = qg_all[:, 0].reshape(FAR, D)
    g_far = qg_all[:, 1].reshape(FAR, D)
    aug_far = aug_all[...].reshape(FAR, 128)
    takes = lax.rem(lane, STEP) == row // PICK
    minus_lse = jnp.where(takes & (lane < 3 * STEP), -1.0, 0.0).astype(bf16)
    minus_dot = jnp.where(takes & (lane >= 3 * STEP) & (lane < 6 * STEP), -1.0, 0.0).astype(bf16)
    own_score = nt(block(k_sel), q_far) + nt(minus_lse, aug_far)
    own_prob = jnp.exp(jnp.where(far_ok & sel_ok, own_score, NEG))
    own_ds = own_prob * (nt(block(v_sel), g_far) + nt(minus_dot, aug_far))
    gk_ref[...] = (gk_acc[...] + place(nn(own_ds.astype(bf16), q_far))).astype(bf16)
    gv_ref[...] = (gv_acc[...] + place(nn(own_prob.astype(bf16), g_far))).astype(bf16)

    for copy in first:
        copy.wait_recv()
    sum_y = w_full[0, pl.ds(pl.multiple_of(y * 96, 96), 96)]
    sum_z = w_full[1, pl.ds(pl.multiple_of(z * 96, 96), 96)]
    sum_x = w_full[2, pl.ds(pl.multiple_of(x * 192, 192), 192)]
    for d in range(NY - 1):
        sum_y = sum_y + r1y[d].astype(f32)
        sum_z = sum_z + r1z[d].astype(f32)
    for d in range(NX - 1):
        sum_x = sum_x + r1x[d].astype(f32)
    a0[...] = sum_y.reshape(NX, 24, 128)
    a1[...] = sum_z.reshape(NX, 24, 128)
    a2[...] = sum_x.reshape(NZ, 24, 128)
    second = []
    for d in (4, 3, 5, 2, 6, 1, 7):
        second.append(
            send(a2.at[lax.rem(z + d, NZ)], r22.at[d - 1], b2_s.at[d - 1], b2_r.at[d - 1], z_peer(d))
        )
        if d < NX:
            to = lax.rem(x + d, NX)
            second.append(send(a0.at[to], r20.at[d - 1], b0_s.at[d - 1], b0_r.at[d - 1], x_peer(d)))
            second.append(send(a1.at[to], r21.at[d - 1], b1_s.at[d - 1], b1_r.at[d - 1], x_peer(d)))
    for copy in second:
        copy.wait_recv()
    sums = [a0[x], a1[x], a2[z]]
    for d in range(NX - 1):
        sums[0] = sums[0] + r20[d]
        sums[1] = sums[1] + r21[d]
    for d in range(NZ - 1):
        sums[2] = sums[2] + r22[d]

    from_z = (z, y, y)
    last = []
    for l in range(3):
        s3[l, 0] = sums[l][0:16].astype(bf16)
        s3[l, 1] = sums[l][8:24].astype(bf16)
        for role in range(2):
            for c_to in range(2):
                to, mine = last_target(l, role, c_to)
                n = (l * 2 + role) * 2 + c_to
                copy = pltpu.make_async_remote_copy(
                    src_ref=s3.at[l, c_to], dst_ref=r3.at[role, from_z[l]],
                    send_sem=f_s.at[n], recv_sem=f_r.at[role, from_z[l]],
                    device_id=to, device_id_type=MESH,
                )
                last.append((copy, mine))

                @pl.when(jnp.logical_not(mine))
                def _(copy=copy):
                    copy.start()

                @pl.when(mine)
                def _(l=l, role=role, c_to=c_to):
                    r3[role, from_z[l]] = s3[l, c_to]

    for role in range(2):

        def arrive(i, carry, role=role):
            who, there, mine = last_source(role, i)

            @pl.when(there & jnp.logical_not(mine))
            def _():
                pltpu.make_async_remote_copy(
                    src_ref=s3.at[0, 0], dst_ref=r3.at[role, i],
                    send_sem=f_s.at[0], recv_sem=f_r.at[role, i],
                    device_id=who, device_id_type=MESH,
                ).wait_recv()

            return carry

        lax.fori_loop(0, NY, arrive, 0)

    blocks = [jnp.sum(r3[role].astype(f32), axis=0) for role in (1, 0)]
    turned = jnp.concatenate([blocks[0].T, blocks[1].T], axis=0)
    w_full[0, 0:256, 0:16] = turned
    mine_rows = w_full[0, pl.ds(pl.multiple_of(128 - 32 * part, 32), 96), 0:16]
    wg_ref[...] = jnp.where(c == 0, mine_rows[:, 0:12], mine_rows[:, 4:16])

    for copy in kv_copies + qg_copies + aug_copies + [gyt_copy, att_copy] + first + second:
        copy.wait_send()
    for copy, mine in last:

        @pl.when(jnp.logical_not(mine))
        def _(copy=copy):
            copy.wait_send()


def body(queries, keys, values, grad_y, lengths, w_out):
    vmem = pl.BlockSpec(memory_space=pltpu.VMEM)
    rows = jax.ShapeDtypeStruct((ROWS, D), bf16)
    dma = pltpu.SemaphoreType.DMA
    return pl.pallas_call(
        kernel,
        out_shape=(rows, rows, rows, rows, jax.ShapeDtypeStruct((96, 12), f32)),
        in_specs=[pl.BlockSpec(memory_space=pltpu.SMEM)] + [vmem] * 5,
        out_specs=(vmem,) * 5,
        scratch_shapes=[
            pltpu.VMEM((NY, 2, PICK, D), bf16),
            pltpu.VMEM((NY, 2, PICK, D), bf16),
            pltpu.VMEM((NY, PICK, 128), bf16),
            pltpu.VMEM((2, D, ROWS), bf16),
            pltpu.VMEM((2, ROWS, D // 2), bf16),
            pltpu.VMEM((ROWS, D // 2), bf16),
            pltpu.VMEM((ROWS, D), bf16),
            pltpu.VMEM((ROWS, D), f32),
            pltpu.VMEM((D, ROWS), bf16),
            pltpu.VMEM((D, ROWS), bf16),
            pltpu.VMEM((ROWS, D), f32),
            pltpu.VMEM((ROWS, D), f32),
            pltpu.VMEM((3, D, 128), f32),
            pltpu.VMEM((NY, 96, 128), bf16),
            pltpu.VMEM((NZ, 96, 128), bf16),
            pltpu.VMEM((NX, 192, 128), bf16),
            pltpu.VMEM((NY - 1, 96, 128), bf16),
            pltpu.VMEM((NZ - 1, 96, 128), bf16),
            pltpu.VMEM((NX - 1, 192, 128), bf16),
            pltpu.VMEM((NX, 24, 128), f32),
            pltpu.VMEM((NX, 24, 128), f32),
            pltpu.VMEM((NZ, 24, 128), f32),
            pltpu.VMEM((NX - 1, 24, 128), f32),
            pltpu.VMEM((NX - 1, 24, 128), f32),
            pltpu.VMEM((NZ - 1, 24, 128), f32),
            pltpu.VMEM((3, 2, 16, 128), bf16),
            pltpu.VMEM((2, NY, 16, 128), bf16),
        ]
        + [dma((NY - 1,))] * 6
        + [dma((2,))] * 2
        + [dma((NY - 1,))] * 2
        + [dma((NZ - 1,))] * 2
        + [dma((NX - 1,))] * 2
        + [dma((NX - 1,))] * 4
        + [dma((NZ - 1,))] * 2
        + [dma((12,)), dma((2, NY))],
        compiler_params=pltpu.CompilerParams(
            collective_id=0, has_side_effects=True, vmem_limit_bytes=48 * 1024 * 1024
        ),
    )(lengths, queries, keys, values, grad_y, w_out)


def solution(mesh):
    split = P(("slide", "seq"), None)
    return jax.shard_map(
        body,
        mesh=mesh,
        in_specs=(split, split, split, split, P("slide"), P()),
        out_specs=(split, split, split, split, P("seq", "slide")),
        check_vma=False,
    )
```

time: 382 us -> 61.4 us (0.16); the launches traced: 376 us -> 60.7 us
  blocking collectives: 130 us -> 0 us
  waiting for transfers between devices: 87.7 us -> 0 us
  local copies, waits for them, and re-layouts: 63.9 us -> 8.9 us
  Pallas kernels: 0 us -> 50.5 us
  starting transfers between devices: 47.3 us -> 0 us
  matrix products: 23.6 us -> 0 us
  between operations: 15.8 us -> 1.3 us
  other arithmetic: 7.62 us -> 0 us
    unnamed x1 -> x0, blocking collectives: 88.1 us -> none
    reduce_scatter x2 -> x0, waiting for transfers between devices: 76.8 us -> none  [the longest x1 42.2 us: body(): lax.psum_scatter(value_part, 'seq', scatter_dimension=0, tiled=True)]
    pallas_call x0 -> x1, Pallas kernels: none -> 50.5 us  [body(): pl.pallas_call(kernel, out_shape=(rows, rows, rows, rows, jax.ShapeDtypeS...]
    unnamed x17 -> x0, starting transfers between devices: 47.2 us -> none
    all_gather x2 -> x0, blocking collectives: 42.3 us -> none  [the longest x1 23.3 us: body(): lax.all_gather(k_sel, 'seq', axis=0, tiled=True)]
    dot_general x15 -> x0, matrix products: 23.6 us -> none  [the longest x1 3.56 us: body(): jnp.einsum('ihd,jhd->hij', q_heads, k_heads, preferred_element_type=f32)]
    unnamed x84 -> x14, local copies, waits for them, and re-layouts: 24.7 us -> 8.23 us
    broadcast_in_dim x11 -> x0, local copies, waits for them, and re-layouts: 13.7 us -> none  [the longest x10 13.7 us: spread_rows(): jnp.where(choose_rows, array_input[:, None], jnp.asarray(filler, array_in...]
  transfers between devices with their start and end apart: 19 -> 0, of which waited for: 3 -> 0; matrix products, arithmetic and copies ran while one was open for 9% -> 0% of each run, Pallas kernels for 0% -> 0%
where the time goes in v1:
time: 61.4 us; the launch traced here: 60.7 us
  Pallas kernels  50.5 us (82%)
  local copies, waits for them, and re-layouts  8.9 us (14%)
  between operations  1.3 us (2%)
    pallas_call x1, Pallas kernels, body(): pl.pallas_call(kernel, out_shape=(rows, rows, rows, rows, jax.ShapeDtypeS...  50.5 us
    unnamed x14, local copies, waits for them, and re-layouts  8.23 us

profile of v1, /device:TPU:1, one launch (start us, length us, event | category | flops | bytes accessed | tf_op | source)
XLA Modules:
  0.0 60.7 jit_solution(14432206561776190167)
XLA Ops:
  1.3 0.0 copy-start
  1.3 1.3 %copy-done = bf16[768,768]{1,0:T(8,128)(2,1)S(1)} copy-done((bf16[768,768]{1,0:T(8,128)(2,1)S(1)}, bf16[768,768]{1,0:T(8,128)(2,1)}, u32[]{:S(2)}) %copy-start) | copy-done | bytes 1179672
  2.6 0.0 copy-start.1
  2.6 1.0 %copy-done.1 = bf16[256,768]{1,0:T(8,128)(2,1)S(1)} copy-done((bf16[256,768]{1,0:T(8,128)(2,1)S(1)}, bf16[256,768]{1,0:T(8,128)(2,1)}, u32[]{:S(2)}) %copy-start.1) | copy-done | bytes 393240
  3.5 0.0 copy-start.2
  3.5 1.0 %copy-done.2 = bf16[256,768]{1,0:T(8,128)(2,1)S(1)} copy-done((bf16[256,768]{1,0:T(8,128)(2,1)S(1)}, bf16[256,768]{1,0:T(8,128)(2,1)}, u32[]{:S(2)}) %copy-start.2) | copy-done | bytes 393240
  4.5 0.0 copy-start.3
  4.5 1.0 %copy-done.3 = bf16[256,768]{1,0:T(8,128)(2,1)S(1)} copy-done((bf16[256,768]{1,0:T(8,128)(2,1)S(1)}, bf16[256,768]{1,0:T(8,128)(2,1)}, u32[]{:S(2)}) %copy-start.3) | copy-done | bytes 393240
  5.5 0.0 copy-start.4
  5.5 1.0 %copy-done.4 = bf16[256,768]{1,0:T(8,128)(2,1)S(1)} copy-done((bf16[256,768]{1,0:T(8,128)(2,1)S(1)}, bf16[256,768]{1,0:T(8,128)(2,1)}, u32[]{:S(2)}) %copy-start.4) | copy-done | bytes 393240
  6.5 50.5 %shard_map.101 = (bf16[256,768]{1,0:T(8,128)(2,1)S(1)}, bf16[256,768]{1,0:T(8,128)(2,1)S(1)}, bf16[256,768]{1,0:T(8,128)(2,1)S(1)}, bf16[256,768]{1,0:T(8,128)(2,1)S(1)}, f32[96,12]{1,0:T(8,128)S(1)}) custom-call(s32[1]{0:T(128)S(6)} %copy.16.len_ref, bf16[256,768]{1,0:T(8,128)(2,1)S(1)} %copy-done.1, bf16[256,768]{1,0:T(8,128)(2,1)S(1)} %copy-done.2, ...), custom_call_target="tpu_custom_call" | custom-call | tf_op jit(solution)/shard_map/pallas_call | solution.py:406
  57.0 0.7 %copy.11 = f32[96,12]{0,1:T(8,128)} copy(f32[96,12]{1,0:T(8,128)S(1)} %get-tuple-element.9) | data formatting | bytes 9216 | tf_op jit(solution)/shard_map/pallas_call | solution.py:406
  57.7 0.7 %copy.17 = bf16[256,768]{1,0:T(8,128)(2,1)} copy(bf16[256,768]{1,0:T(8,128)(2,1)S(1)} %get-tuple-element.15) | data formatting | bytes 786432
  58.5 0.7 %copy.18 = bf16[256,768]{1,0:T(8,128)(2,1)} copy(bf16[256,768]{1,0:T(8,128)(2,1)S(1)} %get-tuple-element.16) | data formatting | bytes 786432
  59.2 0.7 %copy.19 = bf16[256,768]{1,0:T(8,128)(2,1)} copy(bf16[256,768]{1,0:T(8,128)(2,1)S(1)} %get-tuple-element.17) | data formatting | bytes 786432
  59.9 0.7 %copy.20 = bf16[256,768]{1,0:T(8,128)(2,1)} copy(bf16[256,768]{1,0:T(8,128)(2,1)S(1)} %get-tuple-element.18) | data formatting | bytes 786432
Async XLA Ops:
  1.3 1.3 %copy-start = (bf16[768,768]{1,0:T(8,128)(2,1)S(1)}, bf16[768,768]{1,0:T(8,128)(2,1)}, u32[]{:S(2)}) copy-start(bf16[768,768]{1,0:T(8,128)(2,1)} %w_ref.1) | copy-start | bytes 3538948
  2.6 1.0 %copy-start.1 = (bf16[256,768]{1,0:T(8,128)(2,1)S(1)}, bf16[256,768]{1,0:T(8,128)(2,1)}, u32[]{:S(2)}) copy-start(bf16[256,768]{1,0:T(8,128)(2,1)} %q_ref.1) | copy-start | bytes 1179652
  3.5 1.0 %copy-start.2 = (bf16[256,768]{1,0:T(8,128)(2,1)S(1)}, bf16[256,768]{1,0:T(8,128)(2,1)}, u32[]{:S(2)}) copy-start(bf16[256,768]{1,0:T(8,128)(2,1)} %k_ref.1) | copy-start | bytes 1179652
  4.5 1.0 %copy-start.3 = (bf16[256,768]{1,0:T(8,128)(2,1)S(1)}, bf16[256,768]{1,0:T(8,128)(2,1)}, u32[]{:S(2)}) copy-start(bf16[256,768]{1,0:T(8,128)(2,1)} %v_ref.1) | copy-start | bytes 1179652
  5.5 1.0 %copy-start.4 = (bf16[256,768]{1,0:T(8,128)(2,1)S(1)}, bf16[256,768]{1,0:T(8,128)(2,1)}, u32[]{:S(2)}) copy-start(bf16[256,768]{1,0:T(8,128)(2,1)} %gy_ref.1) | copy-start | bytes 1179652

commit v2 on v1

--- a/solution.py
+++ b/solution.py
@@ -1,5 +1,3 @@
-import functools
-
 import jax
 import jax.numpy as jnp
 from jax import lax
@@ -40,15 +38,14 @@
 
 
 def kernel(
-    len_ref, q_ref, k_ref, v_ref, gy_ref, w_ref,
-    out_ref, gq_ref, gk_ref, gv_ref, wg_ref,
+    len_ref, q_hbm, k_hbm, v_hbm, gy_hbm, w_hbm,
+    out_hbm, gq_hbm, gk_hbm, gv_hbm, wg_ref,
+    q_ref, k_ref, v_ref, gy_ref, w_ref, out_ref, gq_ref, gk_ref, gv_ref,
     kv_all, qg_all, aug_all, gyt, atth, att_far,
     grad, att, vt, kt, gk_acc, gv_acc,
-    w_full, wy, wz, wx, r1y, r1z, r1x,
-    a0, a1, a2, r20, r21, r22, s3, r3,
-    kv_s, kv_r, qg_s, qg_r, aug_s, aug_r, core_s, core_r,
-    y_s, y_r, z_s, z_r, x_s, x_r,
-    b0_s, b0_r, b1_s, b1_r, b2_s, b2_r, f_s, f_r,
+    w_full, wz, wx, r1z, r1x, sum_x, a1, a2, r21, r22, s3, r3,
+    in_s, out_s, kv_s, kv_r, qg_s, qg_r, aug_s, aug_r, core_s, core_r,
+    z_s, z_r, x_s, x_r, b1_s, b1_r, b2_s, b2_r, f_s, f_r,
 ):
     slide = lax.axis_index("slide")
     y = lax.axis_index("seq")
@@ -78,26 +75,21 @@
         copy.start()
         return copy
 
-    part = lax.rem(y, 4)
-    src_c = y // 4
-
-    def last_source(role, i):
-        l = part - role
-        at_y = jnp.where(l == 0, z, i)
-        at_z = jnp.where(l == 0, i, jnp.where(l == 1, z, 4 * lax.rem(z, 2) + x))
-        at_x = jnp.where(l == 2, z // 2, x)
-        mine = (at_y == y) & (at_z == z) & (at_x == x) & (src_c == c)
-        there = (l >= 0) & (l <= 2)
-        return device(at_z, at_x, src_c, at_y), there, mine
-
-    def last_target(l, role, c_to):
-        to_y = 4 * c + l + role
-        to_z = (y, z, 2 * x + z // 4)[l]
-        to_x = (x, x, lax.rem(z, 4))[l]
-        mine = (to_y == y) & (to_z == z) & (to_x == x) & (c == c_to)
-        return device(to_z, to_x, c_to, to_y), mine
-
-    r3[...] = jnp.zeros_like(r3)
+    def load(n, src, dst):
+        copy = pltpu.make_async_copy(src, dst, in_s.at[n])
+        copy.start()
+        return copy
+
+    def store(n, src, dst):
+        copy = pltpu.make_async_copy(src, dst, out_s.at[n])
+        copy.start()
+        return copy
+
+    k_in = load(0, k_hbm, k_ref)
+    v_in = load(1, v_hbm, v_ref)
+    gy_in = load(2, gy_hbm, gy_ref)
+    w_in = load(3, w_hbm, w_ref)
+    q_in = load(4, q_hbm, q_ref)
 
     barrier = pltpu.get_barrier_semaphore()
 
@@ -110,24 +102,9 @@
         greet(z_peer(d))
     for d in range(1, NX):
         greet(x_peer(d))
-    greet(sibling)
-    for role in range(2):
-
-        def hail(i, carry, role=role):
-            who, there, mine = last_source(role, i)
-
-            @pl.when(there & jnp.logical_not(mine))
-            def _():
-                greet(who)
-
-            return carry
-
-        lax.fori_loop(0, NY, hail, 0)
-    awaited = (NY - 1) + (NZ - 1) + (NX - 1) + 1
-    for l in range(3):
-        for role in range(2):
-            for c_to in range(2):
-                awaited = awaited + jnp.where(last_target(l, role, c_to)[1], 0, 1)
+    for d in range(NY):
+        greet(device(z, x, 1 - c, lax.rem(y + d, NY)))
+    greeted = (NY - 1) + (NZ - 1) + (NX - 1) + NY
 
     length = len_ref[0]
     base = y * ROWS
@@ -137,21 +114,26 @@
     def compact(rows):
         return nn(squeeze, rows * pick_mask).astype(bf16)
 
+    k_in.wait()
     k_sel = compact(k_ref[...])
+    v_in.wait()
     v_sel = compact(v_ref[...])
     kv_all[y, 0] = k_sel
     kv_all[y, 1] = v_sel
-    gyt[0] = gy_ref[...].T
-
-    pl.semaphore_wait(barrier, awaited)
+
+    pl.semaphore_wait(barrier, greeted)
 
     kv_copies = [
         send(kv_all.at[y], kv_all.at[y], kv_s.at[d - 1], kv_r.at[d - 1], y_peer(d))
         for d in (1, 7, 2, 6, 3, 5, 4)
     ]
+    gy_in.wait()
+    gyt[0] = gy_ref[...].T
     gyt_copy = send(gyt.at[0], gyt.at[1], core_s.at[0], core_r.at[0], sibling)
 
+    w_in.wait()
     grad[...] = nt(gy_ref[...], w_ref[...]).astype(bf16)
+    q_in.wait()
     q_sel = compact(q_ref[...]) * SCALE
     g_sel = compact(grad[...])
     qg_all[y, 0] = q_sel
@@ -268,31 +250,31 @@
         nn(atth[0], w_ref[: D // 2, D // 2 :]) + nn(atth[1], w_ref[D // 2 :, D // 2 :])
     ).astype(bf16)
 
+    stores = [store(0, out_ref, out_hbm)]
+
     gyt_copy.wait_recv()
     att_copy.wait_recv()
     weight = nn(gyt[0], atth[c]) + nn(gyt[1], att_far[...])
     for l in range(3):
-        w_full[l] = weight[:, l * 128 : (l + 1) * 128]
-    wy[...] = w_full[0].reshape(NY, 96, 128).astype(bf16)
+        w_full[l] = weight[:, l * 128 : (l + 1) * 128].reshape(NZ, NX, 24, 128)
     wz[...] = w_full[1].reshape(NZ, 96, 128).astype(bf16)
-    wx[...] = w_full[2].reshape(NX, 192, 128).astype(bf16)
-    first = []
-    for d in (4, 3, 5, 2, 6, 1, 7):
-        first.append(
-            send(wy.at[lax.rem(y + d, NY)], r1y.at[d - 1], y_s.at[d - 1], y_r.at[d - 1], y_peer(d))
-        )
-        first.append(
-            send(wz.at[lax.rem(z + d, NZ)], r1z.at[d - 1], z_s.at[d - 1], z_r.at[d - 1], z_peer(d))
-        )
-        if d < NX:
-            first.append(
-                send(wx.at[lax.rem(x + d, NX)], r1x.at[d - 1], x_s.at[d - 1], x_r.at[d - 1], x_peer(d))
-            )
+    for to in range(NX):
+        for n, l in enumerate((0, 2)):
+            wx[to, n] = w_full[l, :, to].reshape(192, 128).astype(bf16)
+    first_x = [
+        send(wx.at[lax.rem(x + d, NX)], r1x.at[d - 1], x_s.at[d - 1], x_r.at[d - 1], x_peer(d))
+        for d in (2, 1, 3)
+    ]
+    first_z = [
+        send(wz.at[lax.rem(z + d, NZ)], r1z.at[d - 1], z_s.at[d - 1], z_r.at[d - 1], z_peer(d))
+        for d in (4, 3, 5, 2, 6, 1, 7)
+    ]
 
     near_ds = (near_term - near_prob * dot).astype(bf16)
     far_ds = (far_term - far_prob * dot).astype(bf16)
     sel_gq = (nn(near_ds, k_ref[...]) + nn(far_ds, k_far)) * SCALE
     gq_ref[...] = gq_ref[...] + place(sel_gq).astype(bf16)
+    stores.append(store(1, gq_ref, gq_hbm))
     gk_acc[...] += nn(near_ds.astype(f32).T.astype(bf16), q_blk)
     gv_acc[...] += nn(near_prob.T.astype(bf16), g_blk)
 
@@ -312,85 +294,87 @@
     gk_ref[...] = (gk_acc[...] + place(nn(own_ds.astype(bf16), q_far))).astype(bf16)
     gv_ref[...] = (gv_acc[...] + place(nn(own_prob.astype(bf16), g_far))).astype(bf16)
 
-    for copy in first:
-        copy.wait_recv()
-    sum_y = w_full[0, pl.ds(pl.multiple_of(y * 96, 96), 96)]
-    sum_z = w_full[1, pl.ds(pl.multiple_of(z * 96, 96), 96)]
-    sum_x = w_full[2, pl.ds(pl.multiple_of(x * 192, 192), 192)]
-    for d in range(NY - 1):
-        sum_y = sum_y + r1y[d].astype(f32)
-        sum_z = sum_z + r1z[d].astype(f32)
+    stores.append(store(2, gk_ref, gk_hbm))
+    stores.append(store(3, gv_ref, gv_hbm))
+
+    for copy in first_x:
+        copy.wait_recv()
+    for n, l in enumerate((0, 2)):
+        block_sum = w_full[l, :, x]
+        for d in range(NX - 1):
+            block_sum = block_sum + r1x[d, n].astype(f32).reshape(NZ, 24, 128)
+        sum_x[n] = block_sum
+    a2[...] = jnp.concatenate([sum_x[0], sum_x[1]], axis=1).astype(bf16)
+    second_z = [
+        send(a2.at[lax.rem(z + d, NZ)], r22.at[d - 1], b2_s.at[d - 1], b2_r.at[d - 1], z_peer(d))
+        for d in (4, 3, 5, 2, 6, 1, 7)
+    ]
+    for copy in first_z:
+        copy.wait_recv()
+    sum_z = w_full[1, z]
+    for d in range(NZ - 1):
+        sum_z = sum_z + r1z[d].astype(f32).reshape(NX, 24, 128)
+    a1[...] = sum_z
+    second_x = [
+        send(a1.at[lax.rem(x + d, NX)], r21.at[d - 1], b1_s.at[d - 1], b1_r.at[d - 1], x_peer(d))
+        for d in (2, 1, 3)
+    ]
+    for copy in second_x:
+        copy.wait_recv()
+    middle = a1[x]
     for d in range(NX - 1):
-        sum_x = sum_x + r1x[d].astype(f32)
-    a0[...] = sum_y.reshape(NX, 24, 128)
-    a1[...] = sum_z.reshape(NX, 24, 128)
-    a2[...] = sum_x.reshape(NZ, 24, 128)
-    second = []
-    for d in (4, 3, 5, 2, 6, 1, 7):
-        second.append(
-            send(a2.at[lax.rem(z + d, NZ)], r22.at[d - 1], b2_s.at[d - 1], b2_r.at[d - 1], z_peer(d))
-        )
-        if d < NX:
-            to = lax.rem(x + d, NX)
-            second.append(send(a0.at[to], r20.at[d - 1], b0_s.at[d - 1], b0_r.at[d - 1], x_peer(d)))
-            second.append(send(a1.at[to], r21.at[d - 1], b1_s.at[d - 1], b1_r.at[d - 1], x_peer(d)))
-    for copy in second:
-        copy.wait_recv()
-    sums = [a0[x], a1[x], a2[z]]
-    for d in range(NX - 1):
-        sums[0] = sums[0] + r20[d]
-        sums[1] = sums[1] + r21[d]
+        middle = middle + r21[d]
+    for copy in second_z:
+        copy.wait_recv()
+    outer = jnp.concatenate([sum_x[0, z], sum_x[1, z]], axis=0)
     for d in range(NZ - 1):
-        sums[2] = sums[2] + r22[d]
-
-    from_z = (z, y, y)
+        outer = outer + r22[d].astype(f32)
+
+    zero = jnp.zeros((16, 128), bf16)
+    for c_to in range(2):
+        s3[c_to, 0] = zero
+        s3[c_to, 4] = zero
+        for l, rows in enumerate((outer[0:24], middle, outer[24:48])):
+            s3[c_to, l + 1] = rows[8 * c_to : 8 * c_to + 16].astype(bf16)
+    part = lax.rem(y, 4)
     last = []
-    for l in range(3):
-        s3[l, 0] = sums[l][0:16].astype(bf16)
-        s3[l, 1] = sums[l][8:24].astype(bf16)
-        for role in range(2):
-            for c_to in range(2):
-                to, mine = last_target(l, role, c_to)
-                n = (l * 2 + role) * 2 + c_to
-                copy = pltpu.make_async_remote_copy(
-                    src_ref=s3.at[l, c_to], dst_ref=r3.at[role, from_z[l]],
-                    send_sem=f_s.at[n], recv_sem=f_r.at[role, from_z[l]],
-                    device_id=to, device_id_type=MESH,
-                )
-                last.append((copy, mine))
-
-                @pl.when(jnp.logical_not(mine))
-                def _(copy=copy):
-                    copy.start()
-
-                @pl.when(mine)
-                def _(l=l, role=role, c_to=c_to):
-                    r3[role, from_z[l]] = s3[l, c_to]
-
-    for role in range(2):
-
-        def arrive(i, carry, role=role):
-            who, there, mine = last_source(role, i)
-
-            @pl.when(there & jnp.logical_not(mine))
-            def _():
-                pltpu.make_async_remote_copy(
-                    src_ref=s3.at[0, 0], dst_ref=r3.at[role, i],
-                    send_sem=f_s.at[0], recv_sem=f_r.at[role, i],
-                    device_id=who, device_id_type=MESH,
-                ).wait_recv()
-
-            return carry
-
-        lax.fori_loop(0, NY, arrive, 0)
-
-    blocks = [jnp.sum(r3[role].astype(f32), axis=0) for role in (1, 0)]
-    turned = jnp.concatenate([blocks[0].T, blocks[1].T], axis=0)
-    w_full[0, 0:256, 0:16] = turned
-    mine_rows = w_full[0, pl.ds(pl.multiple_of(128 - 32 * part, 32), 96), 0:16]
-    wg_ref[...] = jnp.where(c == 0, mine_rows[:, 0:12], mine_rows[:, 4:16])
-
-    for copy in kv_copies + qg_copies + aug_copies + [gyt_copy, att_copy] + first + second:
+    for t in range(4):
+        for c_to in range(2):
+            mine = (y == 4 * c + t) & (c == c_to)
+            copy = pltpu.make_async_remote_copy(
+                src_ref=s3.at[c_to, pl.ds(t, 2)], dst_ref=r3.at[y],
+                send_sem=f_s.at[2 * t + c_to], recv_sem=f_r.at[y],
+                device_id=device(z, x, c_to, 4 * c + t), device_id_type=MESH,
+            )
+            last.append((copy, mine))
+
+            @pl.when(jnp.logical_not(mine))
+            def _(copy=copy):
+                copy.start()
+
+            @pl.when(mine)
+            def _(t=t, c_to=c_to):
+                r3[y] = s3[c_to, pl.ds(t, 2)]
+
+    for at in range(NY):
+
+        @pl.when(jnp.logical_not((y == at) & (c == y // 4)))
+        def _(at=at):
+            pltpu.make_async_remote_copy(
+                src_ref=s3.at[0, pl.ds(0, 2)], dst_ref=r3.at[at],
+                send_sem=f_s.at[0], recv_sem=f_r.at[at],
+                device_id=device(z, x, y // 4, at), device_id_type=MESH,
+            ).wait_recv()
+
+    both = jnp.sum(r3[...].astype(f32), axis=0)
+    lanes = jnp.concatenate([both[0], both[1]], axis=1)
+    mine_lanes = lanes[:, 128:224]
+    for t in range(1, 4):
+        mine_lanes = jnp.where(part == t, lanes[:, 128 - 32 * t : 224 - 32 * t], mine_lanes)
+    wg_ref[...] = jnp.where(c == 0, mine_lanes[0:12], mine_lanes[4:16])
+
+    sent = kv_copies + qg_copies + aug_copies + [gyt_copy, att_copy]
+    for copy in sent + first_x + first_z + second_x + second_z:
         copy.wait_send()
     for copy, mine in last:
 
@@ -398,17 +382,50 @@
         def _(copy=copy):
             copy.wait_send()
 
+    for copy in stores:
+        copy.wait()
+
+
+def hand_over(*refs):
+    sources, results, held, in_s, out_s = refs[:5], refs[5:10], refs[10:15], refs[15], refs[16]
+    loads = [
+        pltpu.make_async_copy(src, mid, in_s.at[n])
+        for n, (src, mid) in enumerate(zip(sources, held))
+    ]
+    stores = [
+        pltpu.make_async_copy(mid, dst, out_s.at[n])
+        for n, (mid, dst) in enumerate(zip(held, results))
+    ]
+    for copy in loads:
+        copy.start()
+    for arrived, leaving in zip(loads, stores):
+        arrived.wait()
+        leaving.start()
+    for copy in stores:
+        copy.wait()
+
 
 def body(queries, keys, values, grad_y, lengths, w_out):
-    vmem = pl.BlockSpec(memory_space=pltpu.VMEM)
+    hbm = pl.BlockSpec(memory_space=pltpu.HBM)
     rows = jax.ShapeDtypeStruct((ROWS, D), bf16)
     dma = pltpu.SemaphoreType.DMA
-    return pl.pallas_call(
+    shapes = (rows, rows, rows, rows, jax.ShapeDtypeStruct((12, 96), f32))
+    limit = 60 * 1024 * 1024
+    results = pl.pallas_call(
         kernel,
-        out_shape=(rows, rows, rows, rows, jax.ShapeDtypeStruct((96, 12), f32)),
-        in_specs=[pl.BlockSpec(memory_space=pltpu.SMEM)] + [vmem] * 5,
-        out_specs=(vmem,) * 5,
+        out_shape=shapes,
+        in_specs=[pl.BlockSpec(memory_space=pltpu.SMEM)] + [hbm] * 5,
+        out_specs=(hbm,) * 4 + (pl.BlockSpec(memory_space=pltpu.VMEM),),
         scratch_shapes=[
+            pltpu.VMEM((ROWS, D), bf16),
+            pltpu.VMEM((ROWS, D), bf16),
+            pltpu.VMEM((ROWS, D), bf16),
+            pltpu.VMEM((ROWS, D), bf16),
+            pltpu.VMEM((D, D), bf16),
+            pltpu.VMEM((ROWS, D), bf16),
+            pltpu.VMEM((ROWS, D), bf16),
+            pltpu.VMEM((ROWS, D), bf16),
+            pltpu.VMEM((ROWS, D), bf16),
             pltpu.VMEM((NY, 2, PICK, D), bf16),
             pltpu.VMEM((NY, 2, PICK, D), bf16),
             pltpu.VMEM((NY, PICK, 128), bf16),
@@ -421,34 +438,41 @@
             pltpu.VMEM((D, ROWS), bf16),
             pltpu.VMEM((ROWS, D), f32),
             pltpu.VMEM((ROWS, D), f32),
-            pltpu.VMEM((3, D, 128), f32),
-            pltpu.VMEM((NY, 96, 128), bf16),
+            pltpu.VMEM((3, NZ, NX, 24, 128), f32),
             pltpu.VMEM((NZ, 96, 128), bf16),
-            pltpu.VMEM((NX, 192, 128), bf16),
-            pltpu.VMEM((NY - 1, 96, 128), bf16),
+            pltpu.VMEM((NX, 2, 192, 128), bf16),
             pltpu.VMEM((NZ - 1, 96, 128), bf16),
-            pltpu.VMEM((NX - 1, 192, 128), bf16),
+            pltpu.VMEM((NX - 1, 2, 192, 128), bf16),
+            pltpu.VMEM((2, NZ, 24, 128), f32),
             pltpu.VMEM((NX, 24, 128), f32),
-            pltpu.VMEM((NX, 24, 128), f32),
-            pltpu.VMEM((NZ, 24, 128), f32),
+            pltpu.VMEM((NZ, 48, 128), bf16),
             pltpu.VMEM((NX - 1, 24, 128), f32),
-            pltpu.VMEM((NX - 1, 24, 128), f32),
-            pltpu.VMEM((NZ - 1, 24, 128), f32),
-            pltpu.VMEM((3, 2, 16, 128), bf16),
-            pltpu.VMEM((2, NY, 16, 128), bf16),
+            pltpu.VMEM((NZ - 1, 48, 128), bf16),
+            pltpu.VMEM((2, 5, 16, 128), bf16),
+            pltpu.VMEM((NY, 2, 16, 128), bf16),
+            dma((5,)),
+            dma((4,)),
         ]
         + [dma((NY - 1,))] * 6
         + [dma((2,))] * 2
-        + [dma((NY - 1,))] * 2
         + [dma((NZ - 1,))] * 2
-        + [dma((NX - 1,))] * 2
         + [dma((NX - 1,))] * 4
         + [dma((NZ - 1,))] * 2
-        + [dma((12,)), dma((2, NY))],
+        + [dma((8,)), dma((NY,))],
         compiler_params=pltpu.CompilerParams(
-            collective_id=0, has_side_effects=True, vmem_limit_bytes=48 * 1024 * 1024
+            collective_id=0, has_side_effects=True, vmem_limit_bytes=limit
         ),
     )(lengths, queries, keys, values, grad_y, w_out)
+    *grads, weight = pl.pallas_call(
+        hand_over,
+        out_shape=shapes,
+        in_specs=[hbm] * 5,
+        out_specs=(hbm,) * 5,
+        scratch_shapes=[pltpu.VMEM(shape.shape, shape.dtype) for shape in shapes]
+        + [dma((5,)), dma((5,))],
+        compiler_params=pltpu.CompilerParams(vmem_limit_bytes=limit),
+    )(*results)
+    return (*grads, weight.T)
 
 
 def solution(mesh):

time: 61.4 us -> 53.8 us (0.88)
  local copies, waits for them, and re-layouts: 8.9 us -> 0 us
  Pallas kernels: 50.5 us -> 52.3 us
    unnamed x14 -> x0, local copies, waits for them, and re-layouts: 8.23 us -> none
    pallas_call x1 -> x2, Pallas kernels: 50.5 us -> 52.3 us  [the longest x1 50.1 us: body(): pl.pallas_call(kernel, out_shape=shapes, in_specs=[pl.BlockSpec(memory_sp...]
    pallas_call x1 -> x0, local copies, waits for them, and re-layouts: 0.68 us -> none  [body(): pl.pallas_call(kernel, out_shape=(rows, rows, rows, rows, jax.ShapeDtypeS...]
where the time goes in v2:
time: 53.8 us; the launch traced here: 53.6 us
  Pallas kernels  52.3 us (97%)
  between operations  1.29 us (2%)
    pallas_call x1, Pallas kernels, body(): pl.pallas_call(kernel, out_shape=shapes, in_specs=[pl.BlockSpec(memory_sp...  50.1 us
    pallas_call x1, Pallas kernels, body(): pl.pallas_call(hand_over, out_shape=shapes, in_specs=[hbm] * 5, out_specs...  2.22 us

profile of v2, /device:TPU:1, one launch (start us, length us, event | category | flops | bytes accessed | tf_op | source)
XLA Modules:
  0.0 53.6 jit_solution(11701967551190799308)
XLA Ops:
  1.3 50.1 %shard_map.101 = (bf16[256,768]{1,0:T(8,128)(2,1)}, bf16[256,768]{1,0:T(8,128)(2,1)}, bf16[256,768]{1,0:T(8,128)(2,1)}, bf16[256,768]{1,0:T(8,128)(2,1)}, f32[12,96]{1,0:T(8,128)}) custom-call(s32[1]{0:T(128)S(6)} %copy.11.len_ref, bf16[256,768]{1,0:T(8,128)(2,1)} %q_hbm.1, bf16[256,768]{1,0:T(8,128)(2,1)} %k_hbm.1, bf16[256,768]{1,0:T(8,128)(2,1)} %v_hbm.1, ...), custom_call_target="tpu_custom_call" | custom-call | tf_op jit(solution)/shard_map/pallas_call | solution.py:414
  51.4 2.2 %shard_map.102 = (bf16[256,768]{1,0:T(8,128)(2,1)}, bf16[256,768]{1,0:T(8,128)(2,1)}, bf16[256,768]{1,0:T(8,128)(2,1)}, bf16[256,768]{1,0:T(8,128)(2,1)}, f32[12,96]{1,0:T(8,128)}) custom-call(bf16[256,768]{1,0:T(8,128)(2,1)} %get-tuple-element.15.refs_0_, bf16[256,768]{1,0:T(8,128)(2,1)} %get-tuple-element.16.refs_1_, ...), custom_call_target="tpu_custom_call" | custom-call | tf_op jit(solution)/shard_map/pallas_call | solution.py:466

commit v3 on v2

v3 whole, which is shorter than its diff:
```python
import jax
import jax.numpy as jnp
from jax import lax
from jax.experimental import pallas as pl
from jax.experimental.pallas import tpu as pltpu
from jax.sharding import PartitionSpec as P

HD = 64
D = 768
ROWS = 256
STEP = 16
PICK = ROWS // STEP
NY, NZ, NX = 8, 8, 4
FAR = NY * PICK
COMPACT = 4 * PICK
ORDER = (1, 0, 2)
FAR_FIRST = (4, 3, 5, 2, 6, 1, 7)
SCALE = HD**-0.5
NEG = -1e30
MESH = pl.DeviceIdType.MESH
bf16 = jnp.bfloat16
f32 = jnp.float32


def nn(a, b):
    return lax.dot_general(a, b, (((1,), (0,)), ((), ())), preferred_element_type=f32)


def nt(a, b):
    return lax.dot_general(a, b, (((1,), (1,)), ((), ())), preferred_element_type=f32)


def iota(shape, dim):
    return lax.broadcasted_iota(jnp.int32, shape, dim)


def half(cond):
    return jnp.where(cond, 1.0, 0.0).astype(bf16)


def columns(array, l):
    return jnp.concatenate(
        [array[:, 128 * l : 128 * l + 128], array[:, 384 + 128 * l : 512 + 128 * l]], axis=1
    )


def kernel(
    len_ref, q_hbm, k_hbm, v_hbm, gy_hbm, w_hbm,
    out_hbm, gq_hbm, gk_hbm, gv_hbm, wg_ref,
    q_ref, k_ref, v_ref, gy_ref, w_ref, out_ref, gq_ref, gk_ref, gv_ref,
    kv_all, qg_all, aug_all, gyt, atth, att_far,
    grad, att, gk_acc, gv_acc,
    w_full, wz, wx, r1z, r1x, sum_x, a1, a2, r21, r22, s3, r3,
    in_s, out_s, kv_s, kv_r, qg_s, qg_r, aug_s, aug_r, core_s, core_r,
    z_s, z_r, x_s, x_r, b1_s, b1_r, b2_s, b2_r, f_s, f_r,
):
    slide = lax.axis_index("slide")
    y = lax.axis_index("seq")
    c = lax.rem(slide, 2)
    x = lax.rem(slide // 2, NX)
    z = slide // (2 * NX)

    def device(z_at, x_at, c_at, y_at):
        return ((z_at * NX + x_at) * 2 + c_at, y_at)

    def y_peer(d):
        return device(z, x, c, lax.rem(y + d, NY))

    def z_peer(d):
        return device(lax.rem(z + d, NZ), x, c, y)

    def x_peer(d):
        return device(z, lax.rem(x + d, NX), c, y)

    sibling = device(z, x, 1 - c, y)

    def send(src, dst, s_sem, r_sem, to):
        copy = pltpu.make_async_remote_copy(
            src_ref=src, dst_ref=dst, send_sem=s_sem, recv_sem=r_sem,
            device_id=to, device_id_type=MESH,
        )
        copy.start()
        return copy

    def load(n, src, dst):
        copy = pltpu.make_async_copy(src, dst, in_s.at[n])
        copy.start()
        return copy

    def store(n, src, dst):
        copy = pltpu.make_async_copy(src, dst, out_s.at[n])
        copy.start()
        return copy

    k_in = load(0, k_hbm, k_ref)
    v_in = load(1, v_hbm, v_ref)
    gy_in = load(2, gy_hbm, gy_ref)
    w_in = load(3, w_hbm, w_ref)
    q_in = load(4, q_hbm, q_ref)

    barrier = pltpu.get_barrier_semaphore()

    def greet(to):
        pl.semaphore_signal(barrier, inc=1, device_id=to, device_id_type=MESH)

    for d in range(1, NY):
        greet(y_peer(d))
    for d in range(1, NZ):
        greet(z_peer(d))
    for d in range(1, NX):
        greet(x_peer(d))
    for d in range(NY):
        greet(device(z, x, 1 - c, lax.rem(y + d, NY)))
    greeted = (NY - 1) + (NZ - 1) + (NX - 1) + NY

    length = len_ref[0]
    base = y * ROWS
    pick_mask = half(lax.rem(iota((ROWS, D), 0), STEP) == iota((ROWS, D), 1) // HD)
    squeeze = half(iota((PICK, ROWS), 1) // STEP == iota((PICK, ROWS), 0))

    def compact(rows):
        return nn(squeeze, rows * pick_mask).astype(bf16)

    k_in.wait()
    k_sel = compact(k_ref[...])
    v_in.wait()
    v_sel = compact(v_ref[...])
    for l in ORDER:
        kv_all[l, y, 0] = columns(k_sel, l)
        kv_all[l, y, 1] = columns(v_sel, l)

    pl.semaphore_wait(barrier, greeted)

    kv_copies = {}
    for l in ORDER:
        kv_copies[l] = [
            send(
                kv_all.at[l, y], kv_all.at[l, y], kv_s.at[l, d - 1], kv_r.at[l, d - 1], y_peer(d)
            )
            for d in FAR_FIRST
        ]
    gy_in.wait()
    gyt[0] = gy_ref[...].T
    gyt_copy = send(gyt.at[0], gyt.at[1], core_s.at[3], core_r.at[3], sibling)

    w_in.wait()
    grad[...] = nt(gy_ref[...], w_ref[...]).astype(bf16)
    q_in.wait()
    q_sel = compact(q_ref[...]) * SCALE
    g_sel = compact(grad[...])
    qg_all[y, 0] = q_sel
    qg_all[y, 1] = g_sel

    key_ok = base + iota((ROWS, 1), 0) < length
    query_at = iota((1, ROWS), 1)
    query_ok = base + query_at < length

    def dense(l):
        def pair(n, carry):
            p = l + 3 * n
            cols = pl.ds(pl.multiple_of(p * 128, 128), 128)
            k2, v2, q2, g2 = k_ref[:, cols], v_ref[:, cols], q_ref[:, cols] * SCALE, grad[:, cols]
            vt, kt = v2.T, (k2 * SCALE).T
            gk2 = jnp.zeros((ROWS, 128), f32)
            gv2 = jnp.zeros((ROWS, 128), f32)
            tops = []
            for e in range(2):
                lanes = half(iota((1, 128), 1) // HD == e)
                own = slice(e * HD, (e + 1) * HD)
                q_one, g_one = q2 * lanes, g2 * lanes
                score = jnp.where(key_ok, nt(k2, q_one), NEG)
                ex = jnp.exp(score - jnp.max(score, axis=0, keepdims=True))
                total = jnp.sum(ex, axis=0, keepdims=True)
                used = query_ok & (lax.rem(query_at, STEP) != 2 * p + e)
                prob = ex * jnp.where(used, 1.0 / total, 0.0)
                prob_half = prob.astype(bf16)
                term = prob * nt(v2, g_one)
                dot = jnp.sum(term, axis=0, keepdims=True)
                dscore = (term - prob * dot).astype(bf16)
                tops.append((nn(vt[own], prob_half), nn(kt[own], dscore)))
                gk2 = gk2 + nn(dscore, q_one)
                gv2 = gv2 + nn(prob_half, g_one)
            att[:, cols] = jnp.concatenate([tops[0][0], tops[1][0]], axis=0).T
            gq_ref[:, cols] = jnp.concatenate([tops[0][1], tops[1][1]], axis=0).T.astype(bf16)
            gk_acc[:, cols] = gk2
            gv_acc[:, cols] = gv2
            return carry

        lax.fori_loop(0, 2, pair, 0)

    diagonal = half(iota((COMPACT, 256), 0) // PICK == iota((COMPACT, 256), 1) // HD)
    row = iota((COMPACT, 1), 0)
    lane = iota((COMPACT, 128), 1)
    col = iota((ROWS, COMPACT), 1)

    def head_at(l, at):
        return 2 * l + lax.rem(at // PICK, 2) + 6 * (at // (2 * PICK))

    def block(rows):
        return jnp.concatenate([rows] * 4, axis=0) * diagonal

    def spread(l):
        at = iota((ROWS, COMPACT), 0)
        return half((at // STEP == lax.rem(col, PICK)) & (lax.rem(at, STEP) == head_at(l, col)))

    def place(l, rows):
        return nn(spread(l), rows.astype(bf16) * diagonal)

    def oks(l):
        sel_ok = base + lax.rem(row, PICK) * STEP + head_at(l, row) < length
        far_at = lane // PICK * ROWS + lax.rem(lane, PICK) * STEP + head_at(l, row)
        return sel_ok, far_at < length

    def forward(l):
        sel_ok, far_ok = oks(l)
        q_blk, g_blk = block(columns(q_sel, l)), block(columns(g_sel, l))
        k_near, v_near = columns(k_ref, l), columns(v_ref, l)
        near_score = jnp.where(query_ok, nt(q_blk, k_near), NEG)
        near_dprob = nt(g_blk, v_near)
        for copy in kv_copies[l]:
            copy.wait_recv()
        k_far = kv_all[l, :, 0].reshape(FAR, 256)
        v_far = kv_all[l, :, 1].reshape(FAR, 256)
        far_score = jnp.where(far_ok, nt(q_blk, k_far), NEG)
        top = jnp.maximum(
            jnp.max(near_score, axis=1, keepdims=True), jnp.max(far_score, axis=1, keepdims=True)
        )
        near_ex = jnp.exp(near_score - top)
        far_ex = jnp.exp(far_score - top)
        total = jnp.sum(near_ex, axis=1, keepdims=True) + jnp.sum(far_ex, axis=1, keepdims=True)
        inv = jnp.where(sel_ok, 1.0 / total, 0.0)
        near_prob, far_prob = near_ex * inv, far_ex * inv
        sel_att = nn(near_prob.astype(bf16), v_near) + nn(far_prob.astype(bf16), v_far)
        attended = (columns(att, l) + place(l, sel_att)).astype(bf16)
        atth[l, 0] = attended[:, :128]
        atth[l, 1] = attended[:, 128:]
        copy = send(atth.at[l, 1 - c], att_far.at[l], core_s.at[l], core_r.at[l], sibling)
        near_term = near_prob * near_dprob
        far_term = far_prob * nt(g_blk, v_far)
        dot = jnp.sum(near_term, axis=1, keepdims=True) + jnp.sum(far_term, axis=1, keepdims=True)
        aug = jnp.zeros((COMPACT, 128), f32)
        for at, left in ((0, jnp.where(sel_ok, top + jnp.log(total), 0.0)), (3, dot)):
            for n in range(3):
                top_bits = left.astype(bf16).astype(f32)
                aug = jnp.where(lane == (at + n) * STEP + head_at(l, row), top_bits, aug)
                left = left - top_bits
        aug = jnp.sum(aug.reshape(4, PICK, 128), axis=0)
        near_ds = (near_term - near_prob * dot).astype(bf16)
        far_ds = (far_term - far_prob * dot).astype(bf16)
        return copy, attended, aug, (q_blk, g_blk, near_prob, near_ds, far_ds)

    def weight(l, copy):
        copy.wait_recv()
        total = nn(gyt[0], atth[l, c]) + nn(gyt[1], att_far[l])
        w_full[l] = total.reshape(NZ, NX, 24, 128)
        if l == 1:
            wz[...] = total.reshape(NZ, 96, 128).astype(bf16)
            return [
                send(
                    wz.at[lax.rem(z + d, NZ)], r1z.at[d - 1], z_s.at[d - 1], z_r.at[d - 1], z_peer(d)
                )
                for d in FAR_FIRST
            ]
        n = l // 2
        for to in range(NX):
            wx[n, to] = w_full[l, :, to].reshape(192, 128).astype(bf16)
        return [
            send(
                wx.at[n, lax.rem(x + d, NX)], r1x.at[n, d - 1],
                x_s.at[n, d - 1], x_r.at[n, d - 1], x_peer(d),
            )
            for d in (2, 1, 3)
        ]

    dense(1)
    core_1, att_1, aug_1, keep_1 = forward(1)
    dense(0)
    gyt_copy.wait_recv()
    first_z = weight(1, core_1)
    core_0, att_0, aug_0, keep_0 = forward(0)
    dense(2)
    first_0 = weight(0, core_0)
    core_2, att_2, aug_2, keep_2 = forward(2)
    aug_all[y] = (aug_0 + aug_1 + aug_2).astype(bf16)
    qg_copies = [
        send(qg_all.at[y], qg_all.at[y], qg_s.at[d - 1], qg_r.at[d - 1], y_peer(d))
        for d in FAR_FIRST
    ]
    aug_copies = [
        send(aug_all.at[y], aug_all.at[y], aug_s.at[d - 1], aug_r.at[d - 1], y_peer(d))
        for d in FAR_FIRST
    ]
    first_2 = weight(2, core_2)

    def w_rows(l):
        return jnp.concatenate(
            [w_ref[128 * l : 128 * l + 128, :], w_ref[384 + 128 * l : 512 + 128 * l, :]], axis=0
        )

    out_ref[...] = (nn(att_0, w_rows(0)) + nn(att_1, w_rows(1)) + nn(att_2, w_rows(2))).astype(bf16)
    stores = [store(0, out_ref, out_hbm)]

    def put(ref, l, value):
        ref[:, 128 * l : 128 * l + 128] = value[:, :128]
        ref[:, 384 + 128 * l : 512 + 128 * l] = value[:, 128:]

    for l, keep in ((0, keep_0), (1, keep_1), (2, keep_2)):
        q_blk, g_blk, near_prob, near_ds, far_ds = keep
        k_far = kv_all[l, :, 0].reshape(FAR, 256)
        sel_gq = (nn(near_ds, columns(k_ref, l)) + nn(far_ds, k_far)) * SCALE
        put(gq_ref, l, columns(gq_ref, l) + place(l, sel_gq).astype(bf16))
        put(gk_acc, l, columns(gk_acc, l) + nn(near_ds.astype(f32).T.astype(bf16), q_blk))
        put(gv_acc, l, columns(gv_acc, l) + nn(near_prob.T.astype(bf16), g_blk))
    stores.append(store(1, gq_ref, gq_hbm))

    for copy in first_z:
        copy.wait_recv()
    sum_z = w_full[1, z]
    for d in range(NZ - 1):
        sum_z = sum_z + r1z[d].astype(f32).reshape(NX, 24, 128)
    a1[...] = sum_z
    second_x = [
        send(a1.at[lax.rem(x + d, NX)], r21.at[d - 1], b1_s.at[d - 1], b1_r.at[d - 1], x_peer(d))
        for d in (2, 1, 3)
    ]
    second_z = []
    for n, first in enumerate((first_0, first_2)):
        for copy in first:
            copy.wait_recv()
        block_sum = w_full[2 * n, :, x]
        for d in range(NX - 1):
            block_sum = block_sum + r1x[n, d].astype(f32).reshape(NZ, 24, 128)
        sum_x[n] = block_sum
        a2[n] = jnp.concatenate([block_sum, jnp.zeros((NZ, 8, 128), f32)], axis=1).astype(bf16)
        second_z += [
            send(
                a2.at[n, lax.rem(z + d, NZ)], r22.at[n, d - 1],
                b2_s.at[n, d - 1], b2_r.at[n, d - 1], z_peer(d),
            )
            for d in FAR_FIRST
        ]

    for copy in qg_copies:
        copy.wait_recv()
    for copy in aug_copies:
        copy.wait_recv()
    q_far = qg_all[:, 0].reshape(FAR, D)
    g_far = qg_all[:, 1].reshape(FAR, D)
    aug_far = aug_all[...].reshape(FAR, 128)
    for l in range(3):
        sel_ok, far_ok = oks(l)
        takes = lax.rem(lane, STEP) == head_at(l, row)
        minus_lse = jnp.where(takes & (lane < 3 * STEP), -1.0, 0.0).astype(bf16)
        minus_dot = jnp.where(takes & (lane >= 3 * STEP) & (lane < 6 * STEP), -1.0, 0.0).astype(bf16)
        q_l, g_l = columns(q_far, l), columns(g_far, l)
        own_score = nt(block(columns(k_sel, l)), q_l) + nt(minus_lse, aug_far)
        own_prob = jnp.exp(jnp.where(far_ok & sel_ok, own_score, NEG))
        own_ds = own_prob * (nt(block(columns(v_sel, l)), g_l) + nt(minus_dot, aug_far))
        gk_l = columns(gk_acc, l) + place(l, nn(own_ds.astype(bf16), q_l))
        gv_l = columns(gv_acc, l) + place(l, nn(own_prob.astype(bf16), g_l))
        put(gk_ref, l, gk_l.astype(bf16))
        put(gv_ref, l, gv_l.astype(bf16))
    stores.append(store(2, gk_ref, gk_hbm))
    stores.append(store(3, gv_ref, gv_hbm))

    for copy in second_x:
        copy.wait_recv()
    middle = a1[x]
    for d in range(NX - 1):
        middle = middle + r21[d]
    for copy in second_z:
        copy.wait_recv()
    outer = []
    for n in range(2):
        total = sum_x[n, z]
        for d in range(NZ - 1):
            total = total + r22[n, d].astype(f32)[0:24]
        outer.append(total)

    zero = jnp.zeros((16, 128), bf16)
    for c_to in range(2):
        s3[c_to, 0] = zero
        s3[c_to, 4] = zero
        for l, rows in enumerate((outer[0], middle, outer[1])):
            s3[c_to, l + 1] = rows[8 * c_to : 8 * c_to + 16].astype(bf16)
    part = lax.rem(y, 4)
    last = []
    for t in range(4):
        for c_to in range(2):
            mine = (y == 4 * c + t) & (c == c_to)
            copy = pltpu.make_async_remote_copy(
                src_ref=s3.at[c_to, pl.ds(t, 2)], dst_ref=r3.at[y],
                send_sem=f_s.at[2 * t + c_to], recv_sem=f_r.at[y],
                device_id=device(z, x, c_to, 4 * c + t), device_id_type=MESH,
            )
            last.append((copy, mine))

            @pl.when(jnp.logical_not(mine))
            def _(copy=copy):
                copy.start()

            @pl.when(mine)
            def _(t=t, c_to=c_to):
                r3[y] = s3[c_to, pl.ds(t, 2)]

    for at in range(NY):

        @pl.when(jnp.logical_not((y == at) & (c == y // 4)))
        def _(at=at):
            pltpu.make_async_remote_copy(
                src_ref=s3.at[0, pl.ds(0, 2)], dst_ref=r3.at[at],
                send_sem=f_s.at[0], recv_sem=f_r.at[at],
                device_id=device(z, x, y // 4, at), device_id_type=MESH,
            ).wait_recv()

    both = jnp.sum(r3[...].astype(f32), axis=0)
    lanes = jnp.concatenate([both[0], both[1]], axis=1)
    mine_lanes = lanes[:, 128:224]
    for t in range(1, 4):
        mine_lanes = jnp.where(part == t, lanes[:, 128 - 32 * t : 224 - 32 * t], mine_lanes)
    wg_ref[...] = jnp.where(c == 0, mine_lanes[0:12], mine_lanes[4:16])

    sent = kv_copies[0] + kv_copies[1] + kv_copies[2] + qg_copies + aug_copies
    sent += [gyt_copy, core_0, core_1, core_2] + first_z + first_0 + first_2
    for copy in sent + second_x + second_z:
        copy.wait_send()
    for copy, mine in last:

        @pl.when(jnp.logical_not(mine))
        def _(copy=copy):
            copy.wait_send()

    for copy in stores:
        copy.wait()


def hand_over(*refs):
    sources, results, held, in_s, out_s = refs[:5], refs[5:10], refs[10:15], refs[15], refs[16]
    loads = [
        pltpu.make_async_copy(src, mid, in_s.at[n])
        for n, (src, mid) in enumerate(zip(sources, held))
    ]
    stores = [
        pltpu.make_async_copy(mid, dst, out_s.at[n])
        for n, (mid, dst) in enumerate(zip(held, results))
    ]
    for copy in loads:
        copy.start()
    for arrived, leaving in zip(loads, stores):
        arrived.wait()
        leaving.start()
    for copy in stores:
        copy.wait()


def body(queries, keys, values, grad_y, lengths, w_out):
    hbm = pl.BlockSpec(memory_space=pltpu.HBM)
    rows = jax.ShapeDtypeStruct((ROWS, D), bf16)
    dma = pltpu.SemaphoreType.DMA
    shapes = (rows, rows, rows, rows, jax.ShapeDtypeStruct((12, 96), f32))
    limit = 60 * 1024 * 1024
    results = pl.pallas_call(
        kernel,
        out_shape=shapes,
        in_specs=[pl.BlockSpec(memory_space=pltpu.SMEM)] + [hbm] * 5,
        out_specs=(hbm,) * 4 + (pl.BlockSpec(memory_space=pltpu.VMEM),),
        scratch_shapes=[
            pltpu.VMEM((ROWS, D), bf16),
            pltpu.VMEM((ROWS, D), bf16),
            pltpu.VMEM((ROWS, D), bf16),
            pltpu.VMEM((ROWS, D), bf16),
            pltpu.VMEM((D, D), bf16),
            pltpu.VMEM((ROWS, D), bf16),
            pltpu.VMEM((ROWS, D), bf16),
            pltpu.VMEM((ROWS, D), bf16),
            pltpu.VMEM((ROWS, D), bf16),
            pltpu.VMEM((3, NY, 2, PICK, 256), bf16),
            pltpu.VMEM((NY, 2, PICK, D), bf16),
            pltpu.VMEM((NY, PICK, 128), bf16),
            pltpu.VMEM((2, D, ROWS), bf16),
            pltpu.VMEM((3, 2, ROWS, 128), bf16),
            pltpu.VMEM((3, ROWS, 128), bf16),
            pltpu.VMEM((ROWS, D), bf16),
            pltpu.VMEM((ROWS, D), f32),
            pltpu.VMEM((ROWS, D), f32),
            pltpu.VMEM((ROWS, D), f32),
            pltpu.VMEM((3, NZ, NX, 24, 128), f32),
            pltpu.VMEM((NZ, 96, 128), bf16),
            pltpu.VMEM((2, NX, 192, 128), bf16),
            pltpu.VMEM((NZ - 1, 96, 128), bf16),
            pltpu.VMEM((2, NX - 1, 192, 128), bf16),
            pltpu.VMEM((2, NZ, 24, 128), f32),
            pltpu.VMEM((NX, 24, 128), f32),
            pltpu.VMEM((2, NZ, 32, 128), bf16),
            pltpu.VMEM((NX - 1, 24, 128), f32),
            pltpu.VMEM((2, NZ - 1, 32, 128), bf16),
            pltpu.VMEM((2, 5, 16, 128), bf16),
            pltpu.VMEM((NY, 2, 16, 128), bf16),
            dma((5,)),
            dma((4,)),
        ]
        + [dma((3, NY - 1))] * 2
        + [dma((NY - 1,))] * 4
        + [dma((4,))] * 2
        + [dma((NZ - 1,))] * 2
        + [dma((2, NX - 1))] * 2
        + [dma((NX - 1,))] * 2
        + [dma((2, NZ - 1))] * 2
        + [dma((8,)), dma((NY,))],
        compiler_params=pltpu.CompilerParams(
            collective_id=0, has_side_effects=True, vmem_limit_bytes=limit
        ),
    )(lengths, queries, keys, values, grad_y, w_out)
    *grads, weight = pl.pallas_call(
        hand_over,
        out_shape=shapes,
        in_specs=[hbm] * 5,
        out_specs=(hbm,) * 5,
        scratch_shapes=[pltpu.VMEM(shape.shape, shape.dtype) for shape in shapes]
        + [dma((5,)), dma((5,))],
        compiler_params=pltpu.CompilerParams(vmem_limit_bytes=limit),
    )(*results)
    return (*grads, weight.T)


def solution(mesh):
    split = P(("slide", "seq"), None)
    return jax.shard_map(
        body,
        mesh=mesh,
        in_specs=(split, split, split, split, P("slide"), P()),
        out_specs=(split, split, split, split, P("seq", "slide")),
        check_vma=False,
    )
```

time: 53.8 us -> 51.5 us (0.957)
  Pallas kernels: 52.3 us -> 50 us
    pallas_call x1, Pallas kernels: 50.1 us -> 47.8 us  [body(): pl.pallas_call(kernel, out_shape=shapes, in_specs=[pl.BlockSpec(memory_sp...]
where the time goes in v3:
time: 51.5 us; the launch traced here: 51.3 us
  Pallas kernels  50 us (97%)
  between operations  1.29 us (3%)
    pallas_call x1, Pallas kernels, body(): pl.pallas_call(kernel, out_shape=shapes, in_specs=[pl.BlockSpec(memory_sp...  47.8 us
    pallas_call x1, Pallas kernels, body(): pl.pallas_call(hand_over, out_shape=shapes, in_specs=[hbm] * 5, out_specs...  2.22 us

profile of v3, /device:TPU:1, one launch (start us, length us, event | category | flops | bytes accessed | tf_op | source)
XLA Modules:
  0.0 51.3 jit_solution(9997528227583734019)
XLA Ops:
  1.3 47.8 %shard_map.101 = (bf16[256,768]{1,0:T(8,128)(2,1)}, bf16[256,768]{1,0:T(8,128)(2,1)}, bf16[256,768]{1,0:T(8,128)(2,1)}, bf16[256,768]{1,0:T(8,128)(2,1)}, f32[12,96]{1,0:T(8,128)}) custom-call(s32[1]{0:T(128)S(6)} %copy.11.len_ref, bf16[256,768]{1,0:T(8,128)(2,1)} %q_hbm.1, bf16[256,768]{1,0:T(8,128)(2,1)} %k_hbm.1, bf16[256,768]{1,0:T(8,128)(2,1)} %v_hbm.1, ...), custom_call_target="tpu_custom_call" | custom-call | tf_op jit(solution)/shard_map/pallas_call | solution.py:462
  49.1 2.2 %shard_map.102 = (bf16[256,768]{1,0:T(8,128)(2,1)}, bf16[256,768]{1,0:T(8,128)(2,1)}, bf16[256,768]{1,0:T(8,128)(2,1)}, bf16[256,768]{1,0:T(8,128)(2,1)}, f32[12,96]{1,0:T(8,128)}) custom-call(bf16[256,768]{1,0:T(8,128)(2,1)} %get-tuple-element.15.refs_0_, bf16[256,768]{1,0:T(8,128)(2,1)} %get-tuple-element.16.refs_1_, ...), custom_call_target="tpu_custom_call" | custom-call | tf_op jit(solution)/shard_map/pallas_call | solution.py:514

commit v4 on v3

--- a/solution.py
+++ b/solution.py
@@ -92,19 +92,18 @@
         copy.start()
         return copy
 
+    barrier = pltpu.get_barrier_semaphore()
+
+    def greet(to):
+        pl.semaphore_signal(barrier, inc=1, device_id=to, device_id_type=MESH)
+
+    for d in FAR_FIRST:
+        greet(y_peer(d))
     k_in = load(0, k_hbm, k_ref)
     v_in = load(1, v_hbm, v_ref)
     gy_in = load(2, gy_hbm, gy_ref)
     w_in = load(3, w_hbm, w_ref)
     q_in = load(4, q_hbm, q_ref)
-
-    barrier = pltpu.get_barrier_semaphore()
-
-    def greet(to):
-        pl.semaphore_signal(barrier, inc=1, device_id=to, device_id_type=MESH)
-
-    for d in range(1, NY):
-        greet(y_peer(d))
     for d in range(1, NZ):
         greet(z_peer(d))
     for d in range(1, NX):
@@ -250,8 +249,9 @@
         return copy, attended, aug, (q_blk, g_blk, near_prob, near_ds, far_ds)
 
     def weight(l, copy):
+        total = nn(gyt[0], atth[l, c])
         copy.wait_recv()
-        total = nn(gyt[0], atth[l, c]) + nn(gyt[1], att_far[l])
+        total = total + nn(gyt[1], att_far[l])
         w_full[l] = total.reshape(NZ, NX, 24, 128)
         if l == 1:
             wz[...] = total.reshape(NZ, 96, 128).astype(bf16)
@@ -272,15 +272,14 @@
             for d in (2, 1, 3)
         ]
 
-    dense(1)
+    for l in ORDER:
+        dense(l)
     core_1, att_1, aug_1, keep_1 = forward(1)
-    dense(0)
+    core_0, att_0, aug_0, keep_0 = forward(0)
     gyt_copy.wait_recv()
     first_z = weight(1, core_1)
-    core_0, att_0, aug_0, keep_0 = forward(0)
-    dense(2)
+    core_2, att_2, aug_2, keep_2 = forward(2)
     first_0 = weight(0, core_0)
-    core_2, att_2, aug_2, keep_2 = forward(2)
     aug_all[y] = (aug_0 + aug_1 + aug_2).astype(bf16)
     qg_copies = [
         send(qg_all.at[y], qg_all.at[y], qg_s.at[d - 1], qg_r.at[d - 1], y_peer(d))
@@ -332,13 +331,13 @@
             block_sum = block_sum + r1x[n, d].astype(f32).reshape(NZ, 24, 128)
         sum_x[n] = block_sum
         a2[n] = jnp.concatenate([block_sum, jnp.zeros((NZ, 8, 128), f32)], axis=1).astype(bf16)
-        second_z += [
+        second_z.append([
             send(
                 a2.at[n, lax.rem(z + d, NZ)], r22.at[n, d - 1],
                 b2_s.at[n, d - 1], b2_r.at[n, d - 1], z_peer(d),
             )
             for d in FAR_FIRST
-        ]
+        ])
 
     for copy in qg_copies:
         copy.wait_recv()
@@ -363,58 +362,62 @@
     stores.append(store(2, gk_ref, gk_hbm))
     stores.append(store(3, gv_ref, gv_hbm))
 
+    part = lax.rem(y, 4)
+    last = []
+
+    def finish(l, total):
+        for c_to in range(2):
+            s3[l, c_to] = total[8 * c_to : 8 * c_to + 16].astype(bf16)
+        for role in range(2):
+            for c_to in range(2):
+                mine = (y == 4 * c + l + role) & (c == c_to)
+                copy = pltpu.make_async_remote_copy(
+                    src_ref=s3.at[l, c_to], dst_ref=r3.at[role, y],
+                    send_sem=f_s.at[len(last)], recv_sem=f_r.at[role, y],
+                    device_id=device(z, x, c_to, 4 * c + l + role), device_id_type=MESH,
+                )
+                last.append((copy, mine))
+
+                @pl.when(jnp.logical_not(mine))
+                def _(copy=copy):
+                    copy.start()
+
+                @pl.when(mine)
+                def _(l=l, role=role, c_to=c_to):
+                    r3[role, y] = s3[l, c_to]
+
     for copy in second_x:
         copy.wait_recv()
-    middle = a1[x]
+    total = a1[x]
     for d in range(NX - 1):
-        middle = middle + r21[d]
-    for copy in second_z:
-        copy.wait_recv()
-    outer = []
+        total = total + r21[d]
+    finish(1, total)
     for n in range(2):
+        for copy in second_z[n]:
+            copy.wait_recv()
         total = sum_x[n, z]
         for d in range(NZ - 1):
             total = total + r22[n, d].astype(f32)[0:24]
-        outer.append(total)
-
-    zero = jnp.zeros((16, 128), bf16)
-    for c_to in range(2):
-        s3[c_to, 0] = zero
-        s3[c_to, 4] = zero
-        for l, rows in enumerate((outer[0], middle, outer[1])):
-            s3[c_to, l + 1] = rows[8 * c_to : 8 * c_to + 16].astype(bf16)
-    part = lax.rem(y, 4)
-    last = []
-    for t in range(4):
-        for c_to in range(2):
-            mine = (y == 4 * c + t) & (c == c_to)
-            copy = pltpu.make_async_remote_copy(
-                src_ref=s3.at[c_to, pl.ds(t, 2)], dst_ref=r3.at[y],
-                send_sem=f_s.at[2 * t + c_to], recv_sem=f_r.at[y],
-                device_id=device(z, x, c_to, 4 * c + t), device_id_type=MESH,
-            )
-            last.append((copy, mine))
-
-            @pl.when(jnp.logical_not(mine))
-            def _(copy=copy):
-                copy.start()
-
-            @pl.when(mine)
-            def _(t=t, c_to=c_to):
-                r3[y] = s3[c_to, pl.ds(t, 2)]
-
-    for at in range(NY):
-
-        @pl.when(jnp.logical_not((y == at) & (c == y // 4)))
-        def _(at=at):
-            pltpu.make_async_remote_copy(
-                src_ref=s3.at[0, pl.ds(0, 2)], dst_ref=r3.at[at],
-                send_sem=f_s.at[0], recv_sem=f_r.at[at],
-                device_id=device(z, x, y // 4, at), device_id_type=MESH,
-            ).wait_recv()
-
-    both = jnp.sum(r3[...].astype(f32), axis=0)
-    lanes = jnp.concatenate([both[0], both[1]], axis=1)
+        finish(2 * n, total)
+
+    for role in range(2):
+
+        @pl.when((part < role) | (part > role + 2))
+        def _(role=role):
+            r3[role] = jnp.zeros((NY, 16, 128), bf16)
+
+        for at in range(NY):
+
+            @pl.when((part >= role) & (part <= role + 2) & jnp.logical_not((y == at) & (c == y // 4)))
+            def _(role=role, at=at):
+                pltpu.make_async_remote_copy(
+                    src_ref=s3.at[0, 0], dst_ref=r3.at[role, at],
+                    send_sem=f_s.at[0], recv_sem=f_r.at[role, at],
+                    device_id=device(z, x, y // 4, at), device_id_type=MESH,
+                ).wait_recv()
+
+    both = jnp.sum(r3[...].astype(f32), axis=1)
+    lanes = jnp.concatenate([both[1], both[0]], axis=1)
     mine_lanes = lanes[:, 128:224]
     for t in range(1, 4):
         mine_lanes = jnp.where(part == t, lanes[:, 128 - 32 * t : 224 - 32 * t], mine_lanes)
@@ -422,7 +425,7 @@
 
     sent = kv_copies[0] + kv_copies[1] + kv_copies[2] + qg_copies + aug_copies
     sent += [gyt_copy, core_0, core_1, core_2] + first_z + first_0 + first_2
-    for copy in sent + second_x + second_z:
+    for copy in sent + second_x + second_z[0] + second_z[1]:
         copy.wait_send()
     for copy, mine in last:
 
@@ -494,8 +497,8 @@
             pltpu.VMEM((2, NZ, 32, 128), bf16),
             pltpu.VMEM((NX - 1, 24, 128), f32),
             pltpu.VMEM((2, NZ - 1, 32, 128), bf16),
-            pltpu.VMEM((2, 5, 16, 128), bf16),
-            pltpu.VMEM((NY, 2, 16, 128), bf16),
+            pltpu.VMEM((3, 2, 16, 128), bf16),
+            pltpu.VMEM((2, NY, 16, 128), bf16),
             dma((5,)),
             dma((4,)),
         ]
@@ -506,7 +509,7 @@
         + [dma((2, NX - 1))] * 2
         + [dma((NX - 1,))] * 2
         + [dma((2, NZ - 1))] * 2
-        + [dma((8,)), dma((NY,))],
+        + [dma((12,)), dma((2, NY))],
         compiler_params=pltpu.CompilerParams(
             collective_id=0, has_side_effects=True, vmem_limit_bytes=limit
         ),

time: 51.5 us -> 49.2 us (0.955)
  Pallas kernels: 50 us -> 47.7 us
    pallas_call x1, Pallas kernels: 47.8 us -> 45.5 us  [body(): pl.pallas_call(kernel, out_shape=shapes, in_specs=[pl.BlockSpec(memory_sp...]
where the time goes in v4:
time: 49.2 us; the launch traced here: 49 us
  Pallas kernels  47.7 us (97%)
  between operations  1.29 us (3%)
    pallas_call x1, Pallas kernels, body(): pl.pallas_call(kernel, out_shape=shapes, in_specs=[pl.BlockSpec(memory_sp...  45.5 us
    pallas_call x1, Pallas kernels, body(): pl.pallas_call(hand_over, out_shape=shapes, in_specs=[hbm] * 5, out_specs...  2.22 us

profile of v4, /device:TPU:1, one launch (start us, length us, event | category | flops | bytes accessed | tf_op | source)
XLA Modules:
  0.0 49.0 jit_solution(15988251015907668163)
XLA Ops:
  1.3 45.5 %shard_map.101 = (bf16[256,768]{1,0:T(8,128)(2,1)}, bf16[256,768]{1,0:T(8,128)(2,1)}, bf16[256,768]{1,0:T(8,128)(2,1)}, bf16[256,768]{1,0:T(8,128)(2,1)}, f32[12,96]{1,0:T(8,128)}) custom-call(s32[1]{0:T(128)S(6)} %copy.11.len_ref, bf16[256,768]{1,0:T(8,128)(2,1)} %q_hbm.1, bf16[256,768]{1,0:T(8,128)(2,1)} %k_hbm.1, bf16[256,768]{1,0:T(8,128)(2,1)} %v_hbm.1, ...), custom_call_target="tpu_custom_call" | custom-call | tf_op jit(solution)/shard_map/pallas_call | solution.py:465
  46.8 2.2 %shard_map.102 = (bf16[256,768]{1,0:T(8,128)(2,1)}, bf16[256,768]{1,0:T(8,128)(2,1)}, bf16[256,768]{1,0:T(8,128)(2,1)}, bf16[256,768]{1,0:T(8,128)(2,1)}, f32[12,96]{1,0:T(8,128)}) custom-call(bf16[256,768]{1,0:T(8,128)(2,1)} %get-tuple-element.15.refs_0_, bf16[256,768]{1,0:T(8,128)(2,1)} %get-tuple-element.16.refs_1_, ...), custom_call_target="tpu_custom_call" | custom-call | tf_op jit(solution)/shard_map/pallas_call | solution.py:517

commit v5 on v4

--- a/solution.py
+++ b/solution.py
@@ -291,14 +291,6 @@
     ]
     first_2 = weight(2, core_2)
 
-    def w_rows(l):
-        return jnp.concatenate(
-            [w_ref[128 * l : 128 * l + 128, :], w_ref[384 + 128 * l : 512 + 128 * l, :]], axis=0
-        )
-
-    out_ref[...] = (nn(att_0, w_rows(0)) + nn(att_1, w_rows(1)) + nn(att_2, w_rows(2))).astype(bf16)
-    stores = [store(0, out_ref, out_hbm)]
-
     def put(ref, l, value):
         ref[:, 128 * l : 128 * l + 128] = value[:, :128]
         ref[:, 384 + 128 * l : 512 + 128 * l] = value[:, 128:]
@@ -310,7 +302,7 @@
         put(gq_ref, l, columns(gq_ref, l) + place(l, sel_gq).astype(bf16))
         put(gk_acc, l, columns(gk_acc, l) + nn(near_ds.astype(f32).T.astype(bf16), q_blk))
         put(gv_acc, l, columns(gv_acc, l) + nn(near_prob.T.astype(bf16), g_blk))
-    stores.append(store(1, gq_ref, gq_hbm))
+    stores = [store(1, gq_ref, gq_hbm)]
 
     for copy in first_z:
         copy.wait_recv()
@@ -339,6 +331,52 @@
             for d in FAR_FIRST
         ])
 
+    def w_rows(l):
+        return jnp.concatenate(
+            [w_ref[128 * l : 128 * l + 128, :], w_ref[384 + 128 * l : 512 + 128 * l, :]], axis=0
+        )
+
+    out_ref[...] = (nn(att_0, w_rows(0)) + nn(att_1, w_rows(1)) + nn(att_2, w_rows(2))).astype(bf16)
+    stores.append(store(0, out_ref, out_hbm))
+
+    part = lax.rem(y, 4)
+    last = []
+
+    def finish(l, total):
+        for c_to in range(2):
+            s3[l, c_to] = total[8 * c_to : 8 * c_to + 16].astype(bf16)
+        for role in range(2):
+            for c_to in range(2):
+                mine = (y == 4 * c + l + role) & (c == c_to)
+                copy = pltpu.make_async_remote_copy(
+                    src_ref=s3.at[l, c_to], dst_ref=r3.at[role, y],
+                    send_sem=f_s.at[len(last)], recv_sem=f_r.at[role, y],
+                    device_id=device(z, x, c_to, 4 * c + l + role), device_id_type=MESH,
+                )
+                last.append((copy, mine))
+
+                @pl.when(jnp.logical_not(mine))
+                def _(copy=copy):
+                    copy.start()
+
+                @pl.when(mine)
+                def _(l=l, role=role, c_to=c_to):
+                    r3[role, y] = s3[l, c_to]
+
+    for copy in second_x:
+        copy.wait_recv()
+    total = a1[x]
+    for d in range(NX - 1):
+        total = total + r21[d]
+    finish(1, total)
+    for n in range(2):
+        for copy in second_z[n]:
+            copy.wait_recv()
+        total = sum_x[n, z]
+        for d in range(NZ - 1):
+            total = total + r22[n, d].astype(f32)[0:24]
+        finish(2 * n, total)
+
     for copy in qg_copies:
         copy.wait_recv()
     for copy in aug_copies:
@@ -362,44 +400,6 @@
     stores.append(store(2, gk_ref, gk_hbm))
     stores.append(store(3, gv_ref, gv_hbm))
 
-    part = lax.rem(y, 4)
-    last = []
-
-    def finish(l, total):
-        for c_to in range(2):
-            s3[l, c_to] = total[8 * c_to : 8 * c_to + 16].astype(bf16)
-        for role in range(2):
-            for c_to in range(2):
-                mine = (y == 4 * c + l + role) & (c == c_to)
-                copy = pltpu.make_async_remote_copy(
-                    src_ref=s3.at[l, c_to], dst_ref=r3.at[role, y],
-                    send_sem=f_s.at[len(last)], recv_sem=f_r.at[role, y],
-                    device_id=device(z, x, c_to, 4 * c + l + role), device_id_type=MESH,
-                )
-                last.append((copy, mine))
-
-                @pl.when(jnp.logical_not(mine))
-                def _(copy=copy):
-                    copy.start()
-
-                @pl.when(mine)
-                def _(l=l, role=role, c_to=c_to):
-                    r3[role, y] = s3[l, c_to]
-
-    for copy in second_x:
-        copy.wait_recv()
-    total = a1[x]
-    for d in range(NX - 1):
-        total = total + r21[d]
-    finish(1, total)
-    for n in range(2):
-        for copy in second_z[n]:
-            copy.wait_recv()
-        total = sum_x[n, z]
-        for d in range(NZ - 1):
-            total = total + r22[n, d].astype(f32)[0:24]
-        finish(2 * n, total)
-
     for role in range(2):
 
         @pl.when((part < role) | (part > role + 2))
@@ -438,35 +438,28 @@
 
 
 def hand_over(*refs):
-    sources, results, held, in_s, out_s = refs[:5], refs[5:10], refs[10:15], refs[15], refs[16]
-    loads = [
-        pltpu.make_async_copy(src, mid, in_s.at[n])
-        for n, (src, mid) in enumerate(zip(sources, held))
+    copies = [
+        pltpu.make_async_copy(src, dst, refs[10].at[n])
+        for n, (src, dst) in enumerate(zip(refs[:5], refs[5:10]))
     ]
-    stores = [
-        pltpu.make_async_copy(mid, dst, out_s.at[n])
-        for n, (mid, dst) in enumerate(zip(held, results))
-    ]
-    for copy in loads:
+    for copy in copies:
         copy.start()
-    for arrived, leaving in zip(loads, stores):
-        arrived.wait()
-        leaving.start()
-    for copy in stores:
+    for copy in copies:
         copy.wait()
 
 
 def body(queries, keys, values, grad_y, lengths, w_out):
     hbm = pl.BlockSpec(memory_space=pltpu.HBM)
+    anywhere = pl.BlockSpec(memory_space=pl.ANY)
     rows = jax.ShapeDtypeStruct((ROWS, D), bf16)
     dma = pltpu.SemaphoreType.DMA
     shapes = (rows, rows, rows, rows, jax.ShapeDtypeStruct((12, 96), f32))
-    limit = 60 * 1024 * 1024
+    limit = 209 * 1024 * 1024 // 4
     results = pl.pallas_call(
         kernel,
         out_shape=shapes,
         in_specs=[pl.BlockSpec(memory_space=pltpu.SMEM)] + [hbm] * 5,
-        out_specs=(hbm,) * 4 + (pl.BlockSpec(memory_space=pltpu.VMEM),),
+        out_specs=(anywhere,) * 4 + (pl.BlockSpec(memory_space=pltpu.VMEM),),
         scratch_shapes=[
             pltpu.VMEM((ROWS, D), bf16),
             pltpu.VMEM((ROWS, D), bf16),
@@ -517,10 +510,9 @@
     *grads, weight = pl.pallas_call(
         hand_over,
         out_shape=shapes,
-        in_specs=[hbm] * 5,
+        in_specs=[anywhere] * 5,
         out_specs=(hbm,) * 5,
-        scratch_shapes=[pltpu.VMEM(shape.shape, shape.dtype) for shape in shapes]
-        + [dma((5,)), dma((5,))],
+        scratch_shapes=[dma((5,))],
         compiler_params=pltpu.CompilerParams(vmem_limit_bytes=limit),
     )(*results)
     return (*grads, weight.T)

time: 49.2 us -> 47.2 us (0.959)
  Pallas kernels: 47.7 us -> 45.8 us
    pallas_call x1, Pallas kernels: 2.22 us -> 1.18 us  [body(): pl.pallas_call(hand_over, out_shape=shapes, in_specs=[anywhere] * 5, out_...]
    pallas_call x1, Pallas kernels: 45.5 us -> 44.6 us  [body(): pl.pallas_call(kernel, out_shape=shapes, in_specs=[pl.BlockSpec(memory_sp...]
where the time goes in v5:
time: 47.2 us; the launch traced here: 47.1 us
  Pallas kernels  45.8 us (97%)
  between operations  1.29 us (3%)
    pallas_call x1, Pallas kernels, body(): pl.pallas_call(kernel, out_shape=shapes, in_specs=[pl.BlockSpec(memory_sp...  44.6 us
    pallas_call x1, Pallas kernels, body(): pl.pallas_call(hand_over, out_shape=shapes, in_specs=[anywhere] * 5, out_...  1.18 us

profile of v5, /device:TPU:1, one launch (start us, length us, event | category | flops | bytes accessed | tf_op | source)
XLA Modules:
  0.0 47.1 jit_solution(6254284455058912968)
XLA Ops:
  1.3 44.6 %shard_map.101 = (bf16[256,768]{1,0:T(8,128)(2,1)S(1)}, bf16[256,768]{1,0:T(8,128)(2,1)S(1)}, bf16[256,768]{1,0:T(8,128)(2,1)S(1)}, bf16[256,768]{1,0:T(8,128)(2,1)S(1)}, f32[12,96]{1,0:T(8,128)S(1)}) custom-call(s32[1]{0:T(128)S(6)} %copy.11.len_ref, bf16[256,768]{1,0:T(8,128)(2,1)} %q_hbm.1, bf16[256,768]{1,0:T(8,128)(2,1)} %k_hbm.1, ...), custom_call_target="tpu_custom_call" | custom-call | tf_op jit(solution)/shard_map/pallas_call | solution.py:458
  45.9 1.2 %shard_map.102 = (bf16[256,768]{1,0:T(8,128)(2,1)}, bf16[256,768]{1,0:T(8,128)(2,1)}, bf16[256,768]{1,0:T(8,128)(2,1)}, bf16[256,768]{1,0:T(8,128)(2,1)}, f32[12,96]{1,0:T(8,128)}) custom-call(bf16[256,768]{1,0:T(8,128)(2,1)S(1)} %get-tuple-element.15.refs_0_, bf16[256,768]{1,0:T(8,128)(2,1)S(1)} %get-tuple-element.16.refs_1_, ...), custom_call_target="tpu_custom_call" | custom-call | tf_op jit(solution)/shard_map/pallas_call | solution.py:510

commit v6 on v5

--- a/solution.py
+++ b/solution.py
@@ -99,18 +99,18 @@
 
     for d in FAR_FIRST:
         greet(y_peer(d))
+        greet(z_peer(d))
+        greet(device(z, x, 1 - c, lax.rem(y + d, NY)))
+    for d in (2, 1, 3):
+        greet(x_peer(d))
+    greet(sibling)
+    greeted = (NY - 1) + (NZ - 1) + (NX - 1) + NY
+
     k_in = load(0, k_hbm, k_ref)
     v_in = load(1, v_hbm, v_ref)
     gy_in = load(2, gy_hbm, gy_ref)
     w_in = load(3, w_hbm, w_ref)
     q_in = load(4, q_hbm, q_ref)
-    for d in range(1, NZ):
-        greet(z_peer(d))
-    for d in range(1, NX):
-        greet(x_peer(d))
-    for d in range(NY):
-        greet(device(z, x, 1 - c, lax.rem(y + d, NY)))
-    greeted = (NY - 1) + (NZ - 1) + (NX - 1) + NY
 
     length = len_ref[0]
     base = y * ROWS
@@ -215,25 +215,30 @@
         q_blk, g_blk = block(columns(q_sel, l)), block(columns(g_sel, l))
         k_near, v_near = columns(k_ref, l), columns(v_ref, l)
         near_score = jnp.where(query_ok, nt(q_blk, k_near), NEG)
+        near_top = jnp.max(near_score, axis=1, keepdims=True)
+        near_ex = jnp.exp(near_score - near_top)
+        near_total = jnp.sum(near_ex, axis=1, keepdims=True)
+        near_att = nn(near_ex.astype(bf16), v_near)
         near_dprob = nt(g_blk, v_near)
+        spread_l = spread(l)
+        dense_att = columns(att, l)
         for copy in kv_copies[l]:
             copy.wait_recv()
         k_far = kv_all[l, :, 0].reshape(FAR, 256)
         v_far = kv_all[l, :, 1].reshape(FAR, 256)
         far_score = jnp.where(far_ok, nt(q_blk, k_far), NEG)
-        top = jnp.maximum(
-            jnp.max(near_score, axis=1, keepdims=True), jnp.max(far_score, axis=1, keepdims=True)
-        )
-        near_ex = jnp.exp(near_score - top)
+        top = jnp.maximum(near_top, jnp.max(far_score, axis=1, keepdims=True))
+        near_scale = jnp.exp(near_top - top)
         far_ex = jnp.exp(far_score - top)
-        total = jnp.sum(near_ex, axis=1, keepdims=True) + jnp.sum(far_ex, axis=1, keepdims=True)
+        total = near_total * near_scale + jnp.sum(far_ex, axis=1, keepdims=True)
         inv = jnp.where(sel_ok, 1.0 / total, 0.0)
-        near_prob, far_prob = near_ex * inv, far_ex * inv
-        sel_att = nn(near_prob.astype(bf16), v_near) + nn(far_prob.astype(bf16), v_far)
-        attended = (columns(att, l) + place(l, sel_att)).astype(bf16)
+        near_inv = near_scale * inv
+        sel_att = near_att * near_inv + nn(far_ex.astype(bf16), v_far) * inv
+        attended = (dense_att + nn(spread_l, sel_att.astype(bf16) * diagonal)).astype(bf16)
         atth[l, 0] = attended[:, :128]
         atth[l, 1] = attended[:, 128:]
         copy = send(atth.at[l, 1 - c], att_far.at[l], core_s.at[l], core_r.at[l], sibling)
+        near_prob, far_prob = near_ex * near_inv, far_ex * inv
         near_term = near_prob * near_dprob
         far_term = far_prob * nt(g_blk, v_far)
         dot = jnp.sum(near_term, axis=1, keepdims=True) + jnp.sum(far_term, axis=1, keepdims=True)
@@ -262,15 +267,14 @@
                 for d in FAR_FIRST
             ]
         n = l // 2
-        for to in range(NX):
+        copies = []
+        for d in (2, 1, 3):
+            to = lax.rem(x + d, NX)
             wx[n, to] = w_full[l, :, to].reshape(192, 128).astype(bf16)
-        return [
-            send(
-                wx.at[n, lax.rem(x + d, NX)], r1x.at[n, d - 1],
-                x_s.at[n, d - 1], x_r.at[n, d - 1], x_peer(d),
+            copies.append(
+                send(wx.at[n, to], r1x.at[n, d - 1], x_s.at[n, d - 1], x_r.at[n, d - 1], x_peer(d))
             )
-            for d in (2, 1, 3)
-        ]
+        return copies
 
     for l in ORDER:
         dense(l)
@@ -400,6 +404,19 @@
     stores.append(store(2, gk_ref, gk_hbm))
     stores.append(store(3, gv_ref, gv_hbm))
 
+    sent = kv_copies[0] + kv_copies[1] + kv_copies[2] + qg_copies + aug_copies
+    sent += [gyt_copy, core_0, core_1, core_2] + first_z + first_0 + first_2
+    for copy in sent + second_x + second_z[0] + second_z[1]:
+        copy.wait_send()
+    for copy in stores:
+        copy.wait()
+
+    for copy, mine in last:
+
+        @pl.when(jnp.logical_not(mine))
+        def _(copy=copy):
+            copy.wait_send()
+
     for role in range(2):
 
         @pl.when((part < role) | (part > role + 2))
@@ -422,19 +439,6 @@
     for t in range(1, 4):
         mine_lanes = jnp.where(part == t, lanes[:, 128 - 32 * t : 224 - 32 * t], mine_lanes)
     wg_ref[...] = jnp.where(c == 0, mine_lanes[0:12], mine_lanes[4:16])
-
-    sent = kv_copies[0] + kv_copies[1] + kv_copies[2] + qg_copies + aug_copies
-    sent += [gyt_copy, core_0, core_1, core_2] + first_z + first_0 + first_2
-    for copy in sent + second_x + second_z[0] + second_z[1]:
-        copy.wait_send()
-    for copy, mine in last:
-
-        @pl.when(jnp.logical_not(mine))
-        def _(copy=copy):
-            copy.wait_send()
-
-    for copy in stores:
-        copy.wait()
 
 
 def hand_over(*refs):

time: 47.2 us -> 46.4 us (0.983)
  Pallas kernels: 45.8 us -> 45 us
    pallas_call x1, Pallas kernels: 44.6 us -> 43.8 us  [body(): pl.pallas_call(kernel, out_shape=shapes, in_specs=[pl.BlockSpec(memory_sp...]
where the time goes in v6:
time: 46.4 us; the launch traced here: 46.3 us
  Pallas kernels  45 us (97%)
  between operations  1.29 us (3%)
    pallas_call x1, Pallas kernels, body(): pl.pallas_call(kernel, out_shape=shapes, in_specs=[pl.BlockSpec(memory_sp...  43.8 us
    pallas_call x1, Pallas kernels, body(): pl.pallas_call(hand_over, out_shape=shapes, in_specs=[anywhere] * 5, out_...  1.18 us

profile of v6, /device:TPU:1, one launch (start us, length us, event | category | flops | bytes accessed | tf_op | source)
XLA Modules:
  0.0 46.3 jit_solution(13238466187633101274)
XLA Ops:
  1.3 43.8 %shard_map.101 = (bf16[256,768]{1,0:T(8,128)(2,1)S(1)}, bf16[256,768]{1,0:T(8,128)(2,1)S(1)}, bf16[256,768]{1,0:T(8,128)(2,1)S(1)}, bf16[256,768]{1,0:T(8,128)(2,1)S(1)}, f32[12,96]{1,0:T(8,128)S(1)}) custom-call(s32[1]{0:T(128)S(6)} %copy.11.len_ref, bf16[256,768]{1,0:T(8,128)(2,1)} %q_hbm.1, bf16[256,768]{1,0:T(8,128)(2,1)} %k_hbm.1, ...), custom_call_target="tpu_custom_call" | custom-call | tf_op jit(solution)/shard_map/pallas_call | solution.py:462
  45.1 1.2 %shard_map.102 = (bf16[256,768]{1,0:T(8,128)(2,1)}, bf16[256,768]{1,0:T(8,128)(2,1)}, bf16[256,768]{1,0:T(8,128)(2,1)}, bf16[256,768]{1,0:T(8,128)(2,1)}, f32[12,96]{1,0:T(8,128)}) custom-call(bf16[256,768]{1,0:T(8,128)(2,1)S(1)} %get-tuple-element.15.refs_0_, bf16[256,768]{1,0:T(8,128)(2,1)S(1)} %get-tuple-element.16.refs_1_, ...), custom_call_target="tpu_custom_call" | custom-call | tf_op jit(solution)/shard_map/pallas_call | solution.py:514

commit v7 on v6

--- a/solution.py
+++ b/solution.py
@@ -13,7 +13,7 @@
 NY, NZ, NX = 8, 8, 4
 FAR = NY * PICK
 COMPACT = 4 * PICK
-ORDER = (1, 0, 2)
+ORDER = (0, 1, 2)
 FAR_FIRST = (4, 3, 5, 2, 6, 1, 7)
 SCALE = HD**-0.5
 NEG = -1e30
@@ -278,12 +278,12 @@
 
     for l in ORDER:
         dense(l)
+    core_0, att_0, aug_0, keep_0 = forward(0)
     core_1, att_1, aug_1, keep_1 = forward(1)
-    core_0, att_0, aug_0, keep_0 = forward(0)
     gyt_copy.wait_recv()
+    first_0 = weight(0, core_0)
+    core_2, att_2, aug_2, keep_2 = forward(2)
     first_z = weight(1, core_1)
-    core_2, att_2, aug_2, keep_2 = forward(2)
-    first_0 = weight(0, core_0)
     aug_all[y] = (aug_0 + aug_1 + aug_2).astype(bf16)
     qg_copies = [
         send(qg_all.at[y], qg_all.at[y], qg_s.at[d - 1], qg_r.at[d - 1], y_peer(d))
@@ -308,16 +308,6 @@
         put(gv_acc, l, columns(gv_acc, l) + nn(near_prob.T.astype(bf16), g_blk))
     stores = [store(1, gq_ref, gq_hbm)]
 
-    for copy in first_z:
-        copy.wait_recv()
-    sum_z = w_full[1, z]
-    for d in range(NZ - 1):
-        sum_z = sum_z + r1z[d].astype(f32).reshape(NX, 24, 128)
-    a1[...] = sum_z
-    second_x = [
-        send(a1.at[lax.rem(x + d, NX)], r21.at[d - 1], b1_s.at[d - 1], b1_r.at[d - 1], x_peer(d))
-        for d in (2, 1, 3)
-    ]
     second_z = []
     for n, first in enumerate((first_0, first_2)):
         for copy in first:
@@ -335,6 +325,16 @@
             for d in FAR_FIRST
         ])
 
+    for copy in first_z:
+        copy.wait_recv()
+    sum_z = w_full[1, z]
+    for d in range(NZ - 1):
+        sum_z = sum_z + r1z[d].astype(f32).reshape(NX, 24, 128)
+    a1[...] = sum_z
+    second_x = [
+        send(a1.at[lax.rem(x + d, NX)], r21.at[d - 1], b1_s.at[d - 1], b1_r.at[d - 1], x_peer(d))
+        for d in (2, 1, 3)
+    ]
     def w_rows(l):
         return jnp.concatenate(
             [w_ref[128 * l : 128 * l + 128, :], w_ref[384 + 128 * l : 512 + 128 * l, :]], axis=0
@@ -367,19 +367,22 @@
                 def _(l=l, role=role, c_to=c_to):
                     r3[role, y] = s3[l, c_to]
 
+    def finish_z(n):
+        for copy in second_z[n]:
+            copy.wait_recv()
+        total = sum_x[n, z]
+        for d in range(NZ - 1):
+            total = total + r22[n, d].astype(f32)[0:24]
+        finish(2 * n, total)
+
+    finish_z(0)
     for copy in second_x:
         copy.wait_recv()
     total = a1[x]
     for d in range(NX - 1):
         total = total + r21[d]
     finish(1, total)
-    for n in range(2):
-        for copy in second_z[n]:
-            copy.wait_recv()
-        total = sum_x[n, z]
-        for d in range(NZ - 1):
-            total = total + r22[n, d].astype(f32)[0:24]
-        finish(2 * n, total)
+    finish_z(1)
 
     for copy in qg_copies:
         copy.wait_recv()

time: 46.4 us -> 46.2 us (level)
  the two profiles are of different devices: /device:TPU:1 before, /device:TPU:17 now
where the time goes in v7:
time: 46.2 us; the launch traced here: 46.1 us
  Pallas kernels  44.8 us (97%)
  between operations  1.29 us (3%)
    pallas_call x1, Pallas kernels, body(): pl.pallas_call(kernel, out_shape=shapes, in_specs=[pl.BlockSpec(memory_sp...  43.6 us
    pallas_call x1, Pallas kernels, body(): pl.pallas_call(hand_over, out_shape=shapes, in_specs=[anywhere] * 5, out_...  1.18 us

profile of v7, /device:TPU:17, one launch (start us, length us, event | category | flops | bytes accessed | tf_op | source)
XLA Modules:
  0.0 46.1 jit_solution(6951936551885746942)
XLA Ops:
  1.3 43.6 %shard_map.101 = (bf16[256,768]{1,0:T(8,128)(2,1)S(1)}, bf16[256,768]{1,0:T(8,128)(2,1)S(1)}, bf16[256,768]{1,0:T(8,128)(2,1)S(1)}, bf16[256,768]{1,0:T(8,128)(2,1)S(1)}, f32[12,96]{1,0:T(8,128)S(1)}) custom-call(s32[1]{0:T(128)S(6)} %copy.11.len_ref, bf16[256,768]{1,0:T(8,128)(2,1)} %q_hbm.1, bf16[256,768]{1,0:T(8,128)(2,1)} %k_hbm.1, ...), custom_call_target="tpu_custom_call" | custom-call | tf_op jit(solution)/shard_map/pallas_call | solution.py:465
  44.9 1.2 %shard_map.102 = (bf16[256,768]{1,0:T(8,128)(2,1)}, bf16[256,768]{1,0:T(8,128)(2,1)}, bf16[256,768]{1,0:T(8,128)(2,1)}, bf16[256,768]{1,0:T(8,128)(2,1)}, f32[12,96]{1,0:T(8,128)}) custom-call(bf16[256,768]{1,0:T(8,128)(2,1)S(1)} %get-tuple-element.15.refs_0_, bf16[256,768]{1,0:T(8,128)(2,1)S(1)} %get-tuple-element.16.refs_1_, ...), custom_call_target="tpu_custom_call" | custom-call | tf_op jit(solution)/shard_map/pallas_call | solution.py:517
